TPU v7x, 256 devices: a whole 4x4x8 slice. The times are simulated.
256 devices in a mesh: batch: 16 (over z, y_lo), feat: 16 (over y_hi, x, core).
Axes of the slice: x: 4, y: 4 (y_hi: 2, y_lo: 2; y = y_hi * 2 + y_lo), z: 8, core: 2. Of those that a mesh axis runs over, the one named last changes fastest.
Arguments:
- view_a: float32 [16384, 8192], P('batch', 'feat'), may hold values from -1500 to 1500
- view_b: float32 [16384, 8192], P('batch', 'feat'), may hold values from -1500 to 1500
Outputs:
- grad_a: float32 [16384, 8192], P('batch', 'feat')
- grad_b: float32 [16384, 8192], P('batch', 'feat')
- loss: float32 [], replicated
All inputs are finite; a program needn't handle non-finite values.
Results may differ from a plain program's by a relative error of at most 0.0003.
Values sent between devices are 32-bit elements; how exact they have to be, the bound alone decides.
A program may use at most 128 MiB of HBM per device.

v0:
```python
import jax
import jax.numpy as jnp
from jax import lax
from jax.sharding import PartitionSpec as P

BAND = 4


eps = 1e-05
off_weight = 0.25
highest = lax.Precision.HIGHEST


def from_behind(value, axis, steps):
    count = lax.axis_size(axis)
    pairs = [(source, (source + steps) % count) for source in range(count)]
    return lax.ppermute(value, axis, pairs)


def cross_tile(left, right):
    return lax.dot_general(left, right, (((0,), (0,)), ((), ())), precision=highest)


def local(view_a, view_b):
    rows = view_a.shape[0]
    width = view_a.shape[1]
    total = rows * lax.axis_size("batch")
    features = width * lax.axis_size("feat")
    sums = lax.psum((jnp.sum(view_a, 0), jnp.sum(view_b, 0)), "batch")
    cent_a = view_a - sums[0] / total
    cent_b = view_b - sums[1] / total
    spread = lax.psum((jnp.sum(cent_a * cent_a, 0), jnp.sum(cent_b * cent_b, 0)), "batch")
    sd_a = jnp.sqrt(spread[0] / total + eps)
    sd_b = jnp.sqrt(spread[1] / total + eps)
    norm_a = cent_a / sd_a
    norm_b = cent_b / sd_b
    neighbours = [norm_b]
    for step in range(1, BAND):
        neighbours.append(from_behind(neighbours[-1], "feat", -1))
    tiles = [lax.psum(cross_tile(norm_a, block), "batch") / total for block in neighbours]
    diagonal = jnp.diagonal(tiles[0])
    local_loss = jnp.sum((1.0 - diagonal) ** 2) - off_weight * jnp.sum(diagonal * diagonal)
    for tile in tiles:
        local_loss = local_loss + off_weight * jnp.sum(tile * tile)
    loss = lax.psum(local_loss, "feat") / features
    eye = jnp.eye(width, dtype=jnp.float32)
    weights = [off_weight * tile for tile in tiles]
    weights[0] = weights[0] + eye * (-(1.0 - diagonal) - off_weight * diagonal)[None, :]
    g_a = jnp.zeros_like(norm_a)
    for step in range(BAND):
        g_a = g_a + lax.dot_general(
            neighbours[step], weights[step], (((1,), (1,)), ((), ())), precision=highest
        )
    terms = [jnp.dot(norm_a, weights[step], precision=highest) for step in range(BAND)]
    g_b = terms[0]
    for step in range(1, BAND):
        g_b = g_b + from_behind(terms[step], "feat", step)
    back = lax.psum(
        (jnp.sum(g_a, 0), jnp.sum(g_a * norm_a, 0), jnp.sum(g_b, 0), jnp.sum(g_b * norm_b, 0)),
        "batch",
    )
    grad_a = (g_a - back[0] / total - norm_a * (back[1] / total)) / sd_a
    grad_b = (g_b - back[2] / total - norm_b * (back[3] / total)) / sd_b
    return (grad_a, grad_b, loss)


def solution(mesh):
    in_specs = (P("batch", "feat"), P("batch", "feat"))
    out_specs = (P("batch", "feat"), P("batch", "feat"), P())
    return jax.shard_map(local, mesh=mesh, in_specs=in_specs, out_specs=out_specs, check_vma=False)
```

profile of v0, /device:TPU:16, one launch (start us, length us, event | category | flops | bytes accessed | tf_op | source)
XLA Modules:
  0.0 613.4 jit_solution(8282090780655995238)
XLA Ops:
  9.6 37.2 %all-reduce.2 = (f32[512]{0:T(512)S(1)}, f32[512]{0:T(512)S(1)}) all-reduce(f32[512]{0:T(512)S(1)} %reduce_sum.126, f32[512]{0:T(512)S(1)} %reduce_sum.128), channel_id=1, replica_groups=mesh['batch'=16,'feat'=16] {'batch'}, use_global_device_ids=true, to_apply=%region_1.0 | all-reduce | flops 1024 | bytes 8192 | tf_op jit(solution)/shard_map/psum | solution.py:29
  48.9 30.6 %all-reduce.1 = (f32[512]{0:T(512)S(1)}, f32[512]{0:T(512)S(1)}) all-reduce(f32[512]{0:T(512)S(1)} %multiply_reduce_fusion.3, f32[512]{0:T(512)S(1)} %multiply_reduce_fusion.2), channel_id=1, replica_groups=mesh['batch'=16,'feat'=16] {'batch'}, use_global_device_ids=true, to_apply=%region_3.0 | all-reduce | flops 1024 | bytes 8192 | tf_op jit(solution)/shard_map/psum | solution.py:32
  81.5 23.5 %collective-permute-done = f32[1024,512]{1,0:T(8,128)S(1)} collective-permute-done((f32[1024,512]{1,0:T(8,128)S(1)}, f32[1024,512]{1,0:T(8,128)S(1)}, u32[]{:S(2)}, u32[]{:S(2)}) %collective-permute-start) | collective-permute-done | bytes 2097184 | tf_op jit(solution)/shard_map/ppermute | solution.py:17
  105.1 5.5 collective-permute-start.1
  110.6 23.6 %collective-permute-done.1 = f32[1024,512]{1,0:T(8,128)S(1)} collective-permute-done((f32[1024,512]{1,0:T(8,128)S(1)}, f32[1024,512]{1,0:T(8,128)S(1)}, u32[]{:S(2)}, u32[]{:S(2)}) %collective-permute-start.1) | collective-permute-done | bytes 2097184 | tf_op jit(solution)/shard_map/ppermute | solution.py:17
  134.1 5.7 collective-permute-start.2
  139.8 4.6 fusion.37
  144.5 4.6 fusion.36
  149.1 4.6 fusion.35
  153.6 9.7 %collective-permute-done.2 = f32[1024,512]{1,0:T(8,128)S(1)} collective-permute-done((f32[1024,512]{1,0:T(8,128)S(1)}, f32[1024,512]{1,0:T(8,128)S(1)}, u32[]{:S(2)}, u32[]{:S(2)}) %collective-permute-start.2) | collective-permute-done | bytes 2097184 | tf_op jit(solution)/shard_map/ppermute | solution.py:17
  164.7 5.0 fusion.34
  169.7 203.2 %all-reduce.6.cloned.1.call-done = (f32[512,512]{1,0:T(8,128)}, f32[512,512]{1,0:T(8,128)}, f32[512,512]{1,0:T(8,128)}, f32[512,512]{1,0:T(8,128)}) async-done(((f32[512,512]{1,0:T(8,128)}, f32[512,512]{1,0:T(8,128)}, f32[512,512]{1,0:T(8,128)}, f32[512,512]{1,0:T(8,128)}), (f32[512,512]{1,0:T(8,128)}, f32[512,512]{1,0:T(8,128)}, f32[512,512]{1,0:T(8,128)}, ...) | async-done | bytes 4194320 | tf_op jit(solution)/shard_map/psum | solution.py:40
  375.0 6.2 %fusion.7 = f32[1024,512]{1,0:T(8,128)} fusion(f32[512,512]{1,0:T(8,128)} %get-tuple-element.19, f32[1024,512]{1,0:T(8,128)S(1)} %copy-done, f32[512]{0:T(512)S(1)} %add_sqrt_fusion, f32[512]{0:T(512)S(1)} %get-tuple-element.26), kind=kOutput, calls=%fused_computation.24 | convolution fusion | flops 3222536192 | bytes 5246976 | tf_op jit(solution)/shard_map/dot_general | solution.py:54
  382.1 4.9 fusion
  388.3 6.3 %fusion.3 = f32[1024,512]{1,0:T(8,128)} fusion(f32[512,512]{1,0:T(8,128)} %get-tuple-element.17, f32[1024,512]{1,0:T(8,128)S(1)} %copy-done, f32[512]{0:T(512)S(1)} %add_sqrt_fusion, f32[512]{0:T(512)S(1)} %get-tuple-element.26), kind=kOutput, calls=%fused_computation.20 | convolution fusion | flops 3222536192 | bytes 5246976 | tf_op jit(solution)/shard_map/dot_general | solution.py:54
  402.0 8.8 %gather_fusion = f32[512]{0:T(512)S(1)} fusion(f32[512,512]{1,0:T(8,128)} %get-tuple-element.22, s32[512]{0:T(512)S(1)} %bitcast.9), kind=kCustom, calls=%fused_computation | custom fusion | bytes 8192 | tf_op jit(solution)/shard_map/jit(diagonal)/cond/branch_0_fun/gather | solution.py:41
  412.7 127.7 %psum.103 = f32[]{:T(128)} all-reduce(f32[]{:T(128)S(6)} %add.81), channel_id=1, replica_groups=mesh['batch'=16,'feat'=16] {'feat'}, use_global_device_ids=true, to_apply=%region_26.27 | all-reduce | flops 1 | bytes 8 | tf_op jit(solution)/shard_map/psum | solution.py:45
  541.0 5.4 fusion.5
  546.5 3.5 fusion.9
  550.0 3.5 fusion.11
  553.5 5.4 fusion.39
  558.9 7.1 %fusion.38 = (f32[512]{0:T(512)S(1)}, f32[512]{0:T(512)S(1)}, f32[1024,512]{1,0:T(8,128)}) fusion(f32[1024,512]{1,0:T(8,128)S(1)} %copy-done.3, f32[1024,512]{1,0:T(8,128)} %collective-permute-done.5, f32[1024,512]{1,0:T(8,128)} %collective-permute-done.4, f32[1024,512]{1,0:T(8,128)} %collective-permute-done.3, f32[512,512]{1,0:T(8,128)S(1)} %copy-done.4, ...), kind=kOutput, calls=%fused_computation.68 | convolution fusion | flops 3226467328 | bytes 13641728 | tf_op jit(solution)/shard_map/dot_general | solution.py:54
  565.9 33.7 %all-reduce = (f32[512]{0:T(512)S(1)}, f32[512]{0:T(512)S(1)}, f32[512]{0:T(512)S(1)}, f32[512]{0:T(512)S(1)}) all-reduce(f32[512]{0:T(512)S(1)} %get-tuple-element.6, f32[512]{0:T(512)S(1)} %get-tuple-element.5, f32[512]{0:T(512)S(1)} %get-tuple-element.4, f32[512]{0:T(512)S(1)} %get-tuple-element.3), channel_id=1, replica_groups=mesh['batch'=16,'feat'=16] {'batch'}, use_global_device_ids=true, to_apply=%region_15.16 | all-reduce | flops 2048 | bytes 16384 | tf_op jit(solution)/shard_map/psum | solution.py:58
  599.7 3.6 subtract_divide_fusion.1
  (58 shorter events, 19.5 us)
Async XLA Ops:
  7.2 2.2 copy-start
  7.2 365.7 %all-reduce.6.cloned.1.call-start = ((), (), s32[]{:S(2)}) async-start(), calls=%async_computation | async-start | bytes 8388608 | tf_op jit(solution)/shard_map/psum | solution.py:40
  81.4 63.0 %copy-start.2 = (f32[1024,512]{1,0:T(8,128)}, f32[1024,512]{1,0:T(8,128)S(1)}, u32[]{:S(2)}) copy-start(f32[1024,512]{1,0:T(8,128)S(1)} %subtract_divide_fusion.3) | copy-start | bytes 6291460
  81.4 23.6 %collective-permute-start = (f32[1024,512]{1,0:T(8,128)S(1)}, f32[1024,512]{1,0:T(8,128)S(1)}, u32[]{:S(2)}, u32[]{:S(2)}) collective-permute-start(f32[1024,512]{1,0:T(8,128)S(1)} %subtract_divide_fusion.3), channel_id=1, source_target_pairs={{0,15},{1,0},{2,1},{3,2},{4,3},{5,4},{6,5},{7,6},{8,7},{9,8},{10,9... | collective-permute-start | bytes 6291464 | tf_op jit(solution)/shard_map/ppermute | solution.py:17
  105.1 39.4 %copy-start.10 = (f32[1024,512]{1,0:T(8,128)}, f32[1024,512]{1,0:T(8,128)S(1)}, u32[]{:S(2)}) copy-start(f32[1024,512]{1,0:T(8,128)S(1)} %collective-permute-done) | copy-start | bytes 6291460
  105.1 29.1 %collective-permute-start.1 = (f32[1024,512]{1,0:T(8,128)S(1)}, f32[1024,512]{1,0:T(8,128)S(1)}, u32[]{:S(2)}, u32[]{:S(2)}) collective-permute-start(f32[1024,512]{1,0:T(8,128)S(1)} %collective-permute-done), channel_id=1, source_target_pairs={{0,15},{1,0},{2,1},{3,2},{4,3},{5,4},{6,5},{7,6},{8,7},{9,8},{10,9... | collective-permute-start | bytes 6291464 | tf_op jit(solution)/shard_map/ppermute | solution.py:17
  134.1 14.9 %copy-start.12 = (f32[1024,512]{1,0:T(8,128)}, f32[1024,512]{1,0:T(8,128)S(1)}, u32[]{:S(2)}) copy-start(f32[1024,512]{1,0:T(8,128)S(1)} %collective-permute-done.1) | copy-start | bytes 6291460
  134.1 29.2 %collective-permute-start.2 = (f32[1024,512]{1,0:T(8,128)S(1)}, f32[1024,512]{1,0:T(8,128)S(1)}, u32[]{:S(2)}, u32[]{:S(2)}) collective-permute-start(f32[1024,512]{1,0:T(8,128)S(1)} %collective-permute-done.1), channel_id=1, source_target_pairs={{0,15},{1,0},{2,1},{3,2},{4,3},{5,4},{6,5},{7,6},{8,7},{9,8},{10,9... | collective-permute-start | bytes 6291464 | tf_op jit(solution)/shard_map/ppermute | solution.py:17
  163.4 1.3 copy-start.13
  375.0 6.2 %copy-start.6 = (f32[512,512]{1,0:T(8,128)S(1)}, f32[512,512]{1,0:T(8,128)}, u32[]{:S(2)}) copy-start(f32[512,512]{1,0:T(8,128)} %get-tuple-element.20) | copy-start | bytes 3145732
  388.3 6.4 %copy-start.4 = (f32[512,512]{1,0:T(8,128)S(1)}, f32[512,512]{1,0:T(8,128)}, u32[]{:S(2)}) copy-start(f32[512,512]{1,0:T(8,128)} %get-tuple-element.18) | copy-start | bytes 3145732
  394.6 5.2 copy-start.9
  396.4 162.4 %collective-permute-start.5 = (f32[1024,512]{1,0:T(8,128)}, f32[1024,512]{1,0:T(8,128)}, u32[]{:S(2)}, u32[]{:S(2)}) collective-permute-start(f32[1024,512]{1,0:T(8,128)} %fusion), channel_id=1, source_target_pairs={{0,3},{1,4},{2,5},{3,6},{4,7},{5,8},{6,9},{7,10},{8,11},{9,12},{10... | collective-permute-start | bytes 6291464 | tf_op jit(solution)/shard_map/ppermute | solution.py:17
  396.7 162.1 %collective-permute-start.4 = (f32[1024,512]{1,0:T(8,128)}, f32[1024,512]{1,0:T(8,128)}, u32[]{:S(2)}, u32[]{:S(2)}) collective-permute-start(f32[1024,512]{1,0:T(8,128)} %fusion.3), channel_id=1, source_target_pairs={{0,2},{1,3},{2,4},{3,5},{4,6},{5,7},{6,8},{7,9},{8,10},{9,11},{10,... | collective-permute-start | bytes 6291464 | tf_op jit(solution)/shard_map/ppermute | solution.py:17
  398.2 160.7 %collective-permute-start.3 = (f32[1024,512]{1,0:T(8,128)}, f32[1024,512]{1,0:T(8,128)}, u32[]{:S(2)}, u32[]{:S(2)}) collective-permute-start(f32[1024,512]{1,0:T(8,128)} %fusion.7), channel_id=1, source_target_pairs={{0,1},{1,2},{2,3},{3,4},{4,5},{5,6},{6,7},{7,8},{8,9},{9,10},{10,1... | collective-permute-start | bytes 6291464 | tf_op jit(solution)/shard_map/ppermute | solution.py:17
  541.0 5.5 copy-start.8
  541.0 5.5 copy-start.11
  546.5 3.5 copy-start.3
  550.0 3.5 copy-start.7
  550.0 3.5 copy-start.14
  599.7 3.7 copy-start.1
  599.7 3.6 copy-start.5
Sparse Core Ops, SparseCore 0:
  169.8 203.0 all-reduce.5
where the time goes:
time: 617 us; the launch traced here: 613 us
  waiting for transfers between devices  260 us (42%)
  blocking collectives  229 us (37%)
  matrix products  61 us (10%)
  between operations  20.1 us (3%)
  other arithmetic  18 us (3%)
  starting transfers between devices  14.7 us (2%)
  local copies, waits for them, and re-layouts  10.4 us (2%)
    psum x1, waiting for transfers between devices, local(): lax.psum(cross_tile(norm_a, block), 'batch') / total  203 us
    psum x1, blocking collectives, local(): loss = lax.psum(local_loss, 'feat') / features  128 us
    ppermute x6, waiting for transfers between devices, from_behind(): return lax.ppermute(value, axis, pairs)  56.8 us
    psum x1, blocking collectives, local(): sums = lax.psum((jnp.sum(view_a, 0), jnp.sum(view_b, 0)), 'batch')  37.2 us
    psum x1, blocking collectives, local(): lax.psum((jnp.sum(g_a, 0), jnp.sum(g_a * norm_a, 0), jnp.sum(g_b, 0), jnp...  33.7 us
    psum x1, blocking collectives, local(): lax.psum((jnp.sum(cent_a * cent_a, 0), jnp.sum(cent_b * cent_b, 0)), 'bat...  30.6 us
    dot_general x4, matrix products, local(): jnp.dot(norm_a, weights[step], precision=highest)  24.5 us
    dot_general x4, matrix products, cross_tile(): lax.dot_general(left, right, (((0,), (0,)), ((), ())), precision=highest)  18.8 us
  transfers between devices with their start and end apart: 7, of which 4 were waited for; matrix products, arithmetic and copies ran while one was open for 7% of the time, Pallas kernels for 0%

commit v1 on v0

v1 whole, which is shorter than its diff:
```python
import functools

import jax
import jax.numpy as jnp
from jax import lax
from jax.experimental import pallas as pl
from jax.experimental.pallas import tpu as pltpu
from jax.sharding import PartitionSpec as P

MESH = pl.DeviceIdType.MESH
F32 = jnp.float32
BF16 = jnp.bfloat16

eps = 1e-05
off_weight = 0.25

NZ = 8
NX = 4
NY = 4
NF = 16
PARTS = 8
BANDS = 4
HOPS = 4


def mod(value, n):
    return lax.rem(value + n, n)


def split(value):
    hi = value.astype(BF16)
    return hi, (value - hi.astype(F32)).astype(BF16)


def dot3(left, right, transposed=False):
    dims = (((1,), (1 if transposed else 0,)), ((), ()))
    dot = functools.partial(lax.dot_general, dimension_numbers=dims, preferred_element_type=F32)
    return dot(left[0], right[0]) + dot(left[0], right[1]) + dot(left[1], right[0])


def kernel(
    a_hbm, b_hbm, ga_hbm, gb_hbm, loss_ref,
    raw_a, raw_b, at_hi, at_lo, b_hi, b_lo, tiles, rs_p, rs_m, y_recv, fin, cfull, c_hi, c_lo,
    g_a, g_b, relay, st_z, st_y, st_a, st_b, squares, columns, means, l_z, l_send, l_recv,
    in_sem, out_sem, direct_s, direct_r, fwd_s, fwd_r, far_s, far_r, rel_s, rel_r,
    stz_s, stz_r, sty_s, sty_r, stf_s, stf_r, rs_s, rs_r, y_s, y_r, hand_s, hand_r,
    ag_s, ag_r, ay_s, ay_r, lz_s, lz_r, loss_s, loss_r,
):
    rows, width = a_hbm.shape
    part = rows // PARTS
    band = rows // BANDS
    chunk = width // NZ
    half = chunk // 2
    total = float(rows * 2 * NZ)
    features = float(width * NF)

    batch = lax.axis_index("batch")
    feat = lax.axis_index("feat")
    z = lax.div(batch, 2)
    y_lo = lax.rem(batch, 2)
    y = lax.div(feat, 2 * NX) * 2 + y_lo
    x = lax.rem(lax.div(feat, 2), NX)
    core = lax.rem(feat, 2)
    even = core == 0
    odd = core == 1
    first_x = x == 0
    last_x = x == NX - 1
    seam = jnp.logical_or(first_x, last_x)

    def at_feat(f):
        return {"batch": batch, "feat": f}

    def at_z(z_other):
        return {"batch": z_other * 2 + y_lo, "feat": feat}

    def at_xy(x_other, y_other):
        f = lax.div(y_other, 2) * (2 * NX) + x_other * 2 + core
        return {"batch": z * 2 + lax.rem(y_other, 2), "feat": f}

    def neighbour(steps):
        return at_feat(mod(feat + steps, NF))

    def crossed(stride):
        return at_feat(feat + stride - 2 * stride * lax.rem(lax.div(feat, stride), 2))

    other_core = crossed(1)
    other_y = {"batch": batch + 1 - 2 * y_lo, "feat": feat}
    above = at_z(mod(z + 1, NZ))
    below = at_z(mod(z - 1, NZ))
    mirror_x = NX - 1 - x
    ahead_crossed = at_feat(mod(feat + 3 - 2 * core, NF))

    def send(src, dst, s_sem, r_sem, device):
        return pltpu.make_async_remote_copy(
            src_ref=src, dst_ref=dst, send_sem=s_sem, recv_sem=r_sem,
            device_id=device, device_id_type=MESH,
        )

    def landed(dst, r_sem, s_sem):
        send(dst, dst, s_sem, r_sem, other_core).wait_recv()

    load_b = pltpu.make_async_copy(b_hbm, raw_b.at[0], in_sem.at[0])
    load_a = pltpu.make_async_copy(a_hbm, raw_a.at[0], in_sem.at[1])
    load_b.start()
    load_a.start()

    barrier = pltpu.get_barrier_semaphore()
    friends = [neighbour(k) for k in (-3, -2, -1, 1, 2, 3)]
    friends += [crossed(k) for k in (2, 4, 8)]
    friends += [at_z(mod(z + d, NZ)) for d in range(1, NZ)]
    friends += [other_y]
    for friend in friends:
        pl.semaphore_signal(barrier, inc=1, device_id=friend, device_id_type=MESH)

    @pl.when(seam)
    def _():
        for friend in (
            at_xy(mirror_x, mod(y - 1, NY)), at_xy(mirror_x, mod(y + 1, NY)),
            at_xy(x, mod(y - 1, NY)), at_xy(x, mod(y + 1, NY)),
        ):
            pl.semaphore_signal(barrier, inc=1, device_id=friend, device_id_type=MESH)

    pl.semaphore_wait(barrier, jnp.where(seam, len(friends) + 4, len(friends)))


    def piece(c):
        return pl.ds(pl.multiple_of(c * part, part), part)

    def direct(view, c):
        src, raw, steps = ((a_hbm, raw_a, 2), (b_hbm, raw_b, -2))[view]
        return send(
            src.at[piece(c)], raw.at[1, piece(c)], direct_s.at[view, c], direct_r.at[view, c],
            neighbour(steps),
        )

    def to_relay(view, c):
        src = (a_hbm, b_hbm)[view]
        return send(
            src.at[piece(c)], relay.at[c - PARTS // 2], direct_s.at[view, c],
            rel_r.at[c - PARTS // 2], at_xy(mirror_x, mod(y - 1, NY)),
        )

    def from_relay(view, r):
        raw = (raw_a, raw_b)[view]
        c = r + PARTS // 2
        return send(
            relay.at[r], raw.at[1, piece(c)], rel_s.at[r], direct_r.at[view, c],
            at_xy(x, mod(y - 1, NY)),
        )

    for c in (0, 4, 1, 5, 2, 6, 3, 7):
        for view, edge in ((1, first_x), (0, last_x)):
            if c < PARTS // 2:
                direct(view, c).start()
            else:
                @pl.when(edge)
                def _():
                    to_relay(view, c).start()

                @pl.when(jnp.logical_not(edge))
                def _():
                    direct(view, c).start()

    def far_b(src):
        return send(src, raw_b.at[3], far_s.at[1], far_r.at[1], neighbour(-1))

    def far_a(src):
        return send(src, raw_a.at[3], far_s.at[0], far_r.at[0], neighbour(1))

    @pl.when(odd)
    def _():
        far_b(b_hbm).start()

    @pl.when(even)
    def _():
        far_a(a_hbm).start()

    load_b.wait()
    load_a.wait()
    strip = 128
    for view, raw in ((0, raw_a), (1, raw_b)):
        def add_up(i, acc):
            v = raw[0, pl.ds(pl.multiple_of(i * strip, strip), strip), :]
            return acc + jnp.sum(v.reshape(strip // 8, 8, width), axis=0)

        zeros = jnp.zeros((8, width), F32)
        acc = lax.fori_loop(0, rows // strip, add_up, zeros)
        mean = jnp.sum(acc, axis=0, keepdims=True) * (1.0 / rows)

        def add_up_squares(i, carry):
            rest, square = carry
            v = raw[0, pl.ds(pl.multiple_of(i * strip, strip), strip), :] - mean
            v = v.reshape(strip // 8, 8, width)
            return rest + jnp.sum(v, axis=0), square + jnp.sum(v * v, axis=0)

        rest, square = lax.fori_loop(0, rows // strip, add_up_squares, (zeros, zeros))
        st_z[z, pl.ds(3 * view, 1), :] = mean
        st_z[z, pl.ds(3 * view + 1, 1), :] = jnp.sum(square, axis=0, keepdims=True)
        st_z[z, pl.ds(3 * view + 2, 1), :] = jnp.sum(rest, axis=0, keepdims=True)

    def stat_z(d):
        return send(
            st_z.at[z], st_z.at[z], stz_s.at[d], stz_r.at[d], at_z(mod(z + d, NZ))
        )

    for d in range(1, NZ):
        stat_z(d).start()
    for d in range(1, NZ):
        landed(st_z.at[mod(z - d, NZ)], stz_r.at[d], stz_s.at[d])
    for view in (0, 1):
        means_z = [st_z[i, pl.ds(3 * view, 1), :] for i in range(NZ)]
        mean = sum(means_z[1:], means_z[0]) * (1.0 / NZ)
        square = jnp.zeros((1, width), F32)
        rest = jnp.zeros((1, width), F32)
        for i in range(NZ):
            off = means_z[i] - mean
            square = square + (st_z[i, pl.ds(3 * view + 1, 1), :] + float(rows) * off * off)
            rest = rest + (st_z[i, pl.ds(3 * view + 2, 1), :] + float(rows) * off)
        st_y[0, pl.ds(3 * view, 1), :] = mean
        st_y[0, pl.ds(3 * view + 1, 1), :] = square
        st_y[0, pl.ds(3 * view + 2, 1), :] = rest
    stat_y = send(st_y.at[0], st_y.at[1], sty_s, sty_r, other_y)
    stat_y.start()
    stat_y.wait_recv()
    rows_z = float(rows * NZ)
    for view, st in ((0, st_a), (1, st_b)):
        mean0, mean1 = (st_y[i, pl.ds(3 * view, 1), :] for i in (0, 1))
        mean = 0.5 * (mean0 + mean1)
        off0, off1 = mean0 - mean, mean1 - mean
        square = (
            st_y[0, pl.ds(3 * view + 1, 1), :] + st_y[1, pl.ds(3 * view + 1, 1), :]
            + rows_z * (off0 * off0 + off1 * off1)
        )
        rest = (
            st_y[0, pl.ds(3 * view + 2, 1), :] + st_y[1, pl.ds(3 * view + 2, 1), :]
            + rows_z * (off0 + off1)
        )
        inverse = 1.0 / jnp.sqrt(square * (1.0 / total) + eps)
        st[0, pl.ds(0, 1), :] = mean
        st[0, pl.ds(1, 1), :] = inverse
        st[0, pl.ds(2, 1), :] = rest * (1.0 / total) * inverse

    def stat_f(view, k):
        st = (st_a, st_b)[view]
        if k == 2:
            slot = 1
        elif (k == 1) == (view == 1):
            slot = 2 + core
        else:
            slot = 3 - core
        return send(
            st.at[0], st.at[slot], stf_s.at[view, k], stf_r.at[view, slot],
            neighbour(-k if view == 1 else k),
        )

    for k in (2, 1, 3):
        for view in (1, 0):
            stat_f(view, k).start()

    def normal(raw, st, slot, rows_here):
        return (raw[slot, rows_here, :] - st[slot, pl.ds(0, 1), :]) * st[slot, pl.ds(1, 1), :]

    def add_tile(t, c, left_hi, left_lo, first):
        right = (b_hi[...], b_lo[...])
        def rows_of(i, carry):
            here = pl.ds(pl.multiple_of(i * (width // 2), width // 2), width // 2)
            out = dot3((left_hi[c, here, :], left_lo[c, here, :]), right)
            if first:
                tiles[t, here, :] = out
            else:
                tiles[t, here, :] = tiles[t, here, :] + out
            return carry
        lax.fori_loop(0, 2, rows_of, 0)

    def band_of(c):
        return pl.ds(pl.multiple_of(c * band, band), band)

    def turn_a(slot, c, index):
        hi, lo = split(normal(raw_a, st_a, slot, band_of(c)).T)
        at_hi[index] = hi
        at_lo[index] = lo

    def take_b(slot, c):
        hi, lo = split(normal(raw_b, st_b, slot, band_of(c)))
        b_hi[...] = hi
        b_lo[...] = lo

    def clear(t, carry):
        tiles[t] = jnp.zeros((width, width), F32)
        return carry

    lax.fori_loop(0, 4, clear, 0)

    def own_tile(c, carry):
        turn_a(0, c, c)
        take_b(0, c)
        add_tile(0, c, at_hi, at_lo, False)
        return carry

    lax.fori_loop(0, BANDS, own_tile, 0)

    def dest(q):
        return pl.multiple_of(mod(q, NZ) * chunk, chunk)

    def sum_send(t, s):
        if s == 0:
            up = pl.ds(dest(z + HOPS), half)
            down = pl.ds(pl.multiple_of(dest(z + HOPS) + half, half), half)
            up_to, down_to = pl.ds(0, half), pl.ds(half, half)
        else:
            up, down = pl.ds(dest(z + HOPS - s), chunk), pl.ds(dest(z - HOPS + s), chunk)
            up_to = down_to = pl.ds(0, chunk)
        return (
            send(tiles.at[t, up], rs_p.at[t, s, up_to], rs_s.at[0, t, s], rs_r.at[0, t, s], above),
            send(tiles.at[t, down], rs_m.at[t, s, down_to], rs_s.at[1, t, s], rs_r.at[1, t, s], below),
        )

    def sum_start(t, s):
        for copy in sum_send(t, s):
            copy.start()

    def sum_take(t, s):
        for copy in sum_send(t, s):
            copy.wait_recv()
        for recv, q, low in ((rs_p, z + HOPS - 1 - s, 0), (rs_m, z - HOPS + 1 + s, half)):
            if s == 0:
                here = pl.ds(pl.multiple_of(dest(q) + low, half), half)
                tiles[t, here, :] = tiles[t, here, :] + recv[t, s, pl.ds(low, half), :]
            else:
                here = pl.ds(dest(q), chunk)
                tiles[t, here, :] = tiles[t, here, :] + recv[t, s]

    mine = pl.ds(dest(z), chunk)

    def y_copy(t):
        return send(tiles.at[t, mine], y_recv.at[t], y_s.at[t], y_r.at[t], other_y)

    def sum_end(t):
        sum_take(t, HOPS - 1)
        y_copy(t).start()

    def sum_all(t):
        y_copy(t).wait_recv()
        return (tiles[t, mine, :] + y_recv[t]) * (1.0 / total)

    def gather_part(s, mover):
        up, down = z - s - mover, z + s + mover
        if s < HOPS - 1:
            return pl.ds(dest(up), chunk), pl.ds(dest(down), chunk)
        return pl.ds(dest(up), half), pl.ds(pl.multiple_of(dest(down) + half, half), half)

    def gather_send(lane, u, s):
        up, down = gather_part(s, 0)
        return (
            send(cfull.at[u, up], cfull.at[u, up], ag_s.at[0, lane, s], ag_r.at[0, lane, s], above),
            send(cfull.at[u, down], cfull.at[u, down], ag_s.at[1, lane, s], ag_r.at[1, lane, s], below),
        )

    def gather_start(lane, u, s):
        for copy in gather_send(lane, u, s):
            copy.start()

    def across(lane, u, s, i):
        p = gather_part(s, 1)[i]
        return send(cfull.at[u, p], cfull.at[u, p], ay_s.at[i, lane, s], ay_r.at[i, lane, s], other_y)

    def gather_take(lane, u, s):
        for i, p in enumerate(gather_part(s, 1)):
            landed(cfull.at[u, p], ag_r.at[i, lane, s], ag_s.at[i, lane, s])
            if lane < 2:
                across(lane, u, s, i).start()
        if s < HOPS - 1:
            gather_start(lane, u, s + 1)

    def gather_other(lane, u):
        for s in range(HOPS):
            for i in (0, 1):
                across(lane, u, s, i).wait_recv()

    lane_tile = (1 + y_lo, 4 + y_lo, 0, 3 + 3 * core, 6 - 3 * core)
    other_tile = (2 - y_lo, 5 - y_lo)

    def gather(lane, s):
        if s < 0:
            gather_start(lane, lane_tile[lane], 0)
        else:
            gather_take(lane, lane_tile[lane], s)

    hand1 = send(cfull.at[1, mine], cfull.at[4, mine], hand_s.at[0], hand_r.at[4], neighbour(2))
    hand2 = send(cfull.at[2, mine], cfull.at[5, mine], hand_s.at[1], hand_r.at[5], ahead_crossed)
    hand3 = send(fin, cfull.at[3, mine], hand_s.at[2], hand_r.at[3], neighbour(-1))
    hand6 = send(fin, cfull.at[6, mine], hand_s.at[3], hand_r.at[6], neighbour(2))

    def hand_take(u):
        landed(cfull.at[u, mine], hand_r.at[u], hand_s.at[0])

    def when(cond, f, *args):
        @pl.when(cond)
        def _():
            f(*args)

    def sum_step(t, s):
        if s < HOPS - 1:
            sum_take(t, s)
            sum_start(t, s + 1)
        else:
            sum_end(t)

    def end_0():
        cfull[0, mine, :] = sum_all(0)

    def end_1():
        cfull[1, mine, :] = sum_all(1)
        hand1.start()

    def end_2():
        cfull[2, mine, :] = sum_all(2)
        hand2.start()

    def end_3_odd():
        last = sum_all(3)
        fin[...] = last
        hand3.start()
        cfull[6, mine, :] = last

    def end_3_even():
        fin[...] = sum_all(3)
        hand3.start()
        hand6.start()

    def forward(view, c):
        raw = (raw_a, raw_b)[view]
        return send(
            raw.at[1, piece(c)], raw.at[2, piece(c)], fwd_s.at[view, c], fwd_r.at[view, c],
            other_core,
        )

    sum_start(0, 0)
    for slot in (3, 1, 2):
        for view, st in ((1, st_b), (0, st_a)):
            landed(st.at[slot], stf_r.at[view, slot], stf_s.at[view, slot])

    @pl.when(odd)
    def _():
        far_a(a_hbm).wait_recv()

        def fourth_tile(c, carry):
            turn_a(3, c, BANDS)
            take_b(0, c)
            add_tile(3, BANDS, at_hi, at_lo, False)
            return carry

        lax.fori_loop(0, BANDS, fourth_tile, 0)
        sum_start(3, 0)

    def early(j):
        if j < HOPS:
            sum_step(0, j)
            when(odd, sum_step, 3, j)
        elif j == 4:
            end_0()
            gather(2, -1)
            when(odd, end_3_odd)
        elif j == 5:
            gather(2, 0)
            when(even, hand_take, 3)
            gather(3, -1)
        else:
            gather(2, j - 5)
            gather(3, j - 6)

    for c in range(BANDS):
        for j in (2 * c, 2 * c + 1):
            if j < PARTS // 2:
                for view, edge in ((1, last_x), (0, first_x)):
                    @pl.when(edge)
                    def _():
                        landed(relay.at[j], rel_r.at[j], rel_s.at[j])
                        from_relay(view, j).start()

            for view in (1, 0):
                direct(view, j).wait_recv()
                forward(view, j).start()
            early(j)
        take_b(1, c)
        add_tile(1, c, at_hi, at_lo, False)

        @pl.when(even)
        def _():
            for j in (2 * c, 2 * c + 1):
                forward(0, j).wait_recv()
            turn_a(2, c, BANDS)
            add_tile(3, BANDS, at_hi, at_lo, False)

        for j in (2 * c, 2 * c + 1):
            forward(1, j).wait_recv()
        take_b(2, c)
        add_tile(2, c, at_hi, at_lo, False)

    @pl.when(odd)
    def _():
        for j in range(PARTS):
            forward(0, j).wait_recv()

    for t in (1, 2):
        sum_start(t, 0)
    when(even, sum_start, 3, 0)
    when(even, far_b(raw_b.at[1]).start)
    when(odd, far_a(raw_a.at[1]).start)

    squares[...] = jnp.zeros_like(squares)
    columns[...] = jnp.zeros_like(columns)
    means[...] = jnp.zeros_like(means)

    def clear_g(i, carry):
        g_a[band_of(i), :] = jnp.zeros((band, width), F32)
        g_b[band_of(i), :] = jnp.zeros((band, width), F32)
        return carry

    lax.fori_loop(0, BANDS, clear_g, 0)

    def grow(view, slot, u):
        g, raw, st = ((g_a, raw_b, st_b), (g_b, raw_a, st_a))[view]
        c = cfull[u]
        hi, lo = split(c)
        c_hi[...] = hi
        c_lo[...] = lo
        if view == 0:
            acc = squares[...]
            for j in range(width // 128):
                part_j = c[:, j * 128:(j + 1) * 128]
                acc = acc + part_j * part_j
            squares[...] = acc
        else:
            columns[...] = columns[...] + jnp.sum((c * c).reshape(width // 8, 8, width), axis=0)

        def body(i, carry):
            here = band_of(i)
            n = split(normal(raw, st, slot, here))
            g[here, :] = g[here, :] + dot3(n, (c_hi[...], c_lo[...]), view == 0)
            return carry

        lax.fori_loop(0, BANDS, body, 0)
        m = split(jnp.broadcast_to(st[slot, pl.ds(2, 1), :], (16, width)))
        means[view] = means[view] + dot3(m, (c_hi[...], c_lo[...]), view == 0)

    def loss_part():
        value = jnp.zeros((8, 128), F32)
        for t in range(4):
            c = fin[...] if t == 3 else cfull[t, mine, :]
            terms = off_weight * c * c
            if t == 0:
                shape = (chunk, width)
                on = lax.broadcasted_iota(jnp.int32, shape, 1) == (
                    lax.broadcasted_iota(jnp.int32, shape, 0) + z * chunk
                )
                terms = jnp.where(on, (1.0 - c) * (1.0 - c), terms)
            terms = jnp.sum(terms.reshape(chunk // 8, 8, width), axis=0)
            for j in range(width // 128):
                value = value + terms[:, j * 128:(j + 1) * 128]
        l_z[z] = value

    def loss_z(d):
        return send(l_z.at[z], l_z.at[z], lz_s.at[d], lz_r.at[d], at_z(mod(z + d, NZ)))

    def loss_copy(r):
        return send(l_send.at[r], l_recv.at[r], loss_s.at[r], loss_r.at[r], crossed(1 << r))

    def loss_start():
        for d in range(1, NZ):
            landed(l_z.at[mod(z - d, NZ)], lz_r.at[d], lz_s.at[d])
        value = l_z[0]
        for i in range(1, NZ):
            value = value + l_z[i]
        l_send[0] = value
        loss_copy(0).start()

    def loss_step(r):
        loss_copy(r).wait_recv()
        l_send[r + 1] = l_send[r] + l_recv[r]
        if r < 3:
            loss_copy(r + 1).start()

    gather(2, 3)
    gather(3, 2)
    grow(0, 0, 0)
    gather(3, 3)
    for t in (1, 2):
        sum_step(t, 0)
    when(even, sum_step, 3, 0)
    grow(1, 0, 0)
    for t in (1, 2):
        sum_step(t, 1)
    when(even, sum_step, 3, 1)
    far_b_here = far_b(raw_b.at[1])
    far_a_here = far_a(raw_a.at[1])

    @pl.when(even)
    def _():
        far_b_here.wait_recv()
        grow(0, 3, 3)

    when(odd, grow, 1, 3, 6)
    for s in (2, 3):
        for t in (1, 2):
            sum_step(t, s)
        when(even, sum_step, 3, s)
    end_1()
    end_2()
    gather(0, -1)
    when(even, end_3_even)
    loss_part()
    for d in range(1, NZ):
        loss_z(d).start()
    hand_take(4)
    hand_take(5)
    gather(1, -1)
    gather(0, 0)
    when(even, hand_take, 6)
    when(odd, hand_take, 3)
    gather(4, -1)
    gather(1, 0)
    gather(0, 1)
    gather(4, 0)
    gather(1, 1)
    gather(0, 2)
    loss_start()
    gather(4, 1)
    gather(1, 2)
    gather(0, 3)
    grow(0, 1 + y_lo, lane_tile[0])
    loss_step(0)
    gather(4, 2)
    gather(1, 3)
    grow(1, 1 + y_lo, lane_tile[1])
    loss_step(1)
    gather(4, 3)
    gather_other(0, other_tile[0])
    grow(0, 2 - y_lo, other_tile[0])
    loss_step(2)
    gather_other(1, other_tile[1])
    grow(1, 2 - y_lo, other_tile[1])
    loss_step(3)

    @pl.when(odd)
    def _():
        far_b_here.wait_recv()
        grow(0, 3, 3)

    @pl.when(even)
    def _():
        far_a_here.wait_recv()
        grow(1, 3, 6)

    loss_ref[0, 0] = jnp.sum(l_send[4]) * (1.0 / features)

    diagonal = []
    one_block = (
        lax.broadcasted_iota(jnp.int32, (128, 128), 0) == lax.broadcasted_iota(jnp.int32, (128, 128), 1)
    )
    for j in range(width // 128):
        block = cfull[0, j * 128:(j + 1) * 128, j * 128:(j + 1) * 128]
        diagonal.append(jnp.sum(jnp.where(one_block, block, 0.0), axis=0, keepdims=True))
    diagonal = jnp.concatenate(diagonal, axis=1)
    change = -(1.0 - diagonal) - off_weight * diagonal
    row_squares = jnp.sum(squares[...].T, axis=0, keepdims=True)
    column_squares = jnp.sum(columns[...], axis=0, keepdims=True)
    back_a = off_weight * row_squares + change * diagonal
    back_b = off_weight * column_squares + change * diagonal
    mean_a = off_weight * means[0, pl.ds(0, 1), :] + st_b[0, pl.ds(2, 1), :] * change
    mean_b = off_weight * means[1, pl.ds(0, 1), :] + st_a[0, pl.ds(2, 1), :] * change

    def out_copy(view, i):
        src, dst = ((g_a, ga_hbm), (g_b, gb_hbm))[view]
        return pltpu.make_async_copy(src.at[band_of(i)], dst.at[band_of(i)], out_sem.at[view, i])

    def finish(i, carry):
        here = band_of(i)
        n_a = normal(raw_a, st_a, 0, here)
        n_b = normal(raw_b, st_b, 0, here)
        g_a[here, :] = (off_weight * g_a[here, :] + n_b * change - mean_a - n_a * back_a) * st_a[0, pl.ds(1, 1), :]
        out_copy(0, i).start()
        g_b[here, :] = (off_weight * g_b[here, :] + n_a * change - mean_b - n_b * back_b) * st_b[0, pl.ds(1, 1), :]
        out_copy(1, i).start()
        return carry

    lax.fori_loop(0, BANDS, finish, 0)

    for view, edge in ((1, first_x), (0, last_x)):
        for c in range(PARTS):
            direct(view, c).wait_send()
            forward(view, c).wait_send()
    far_a(a_hbm).wait_send()
    far_b(b_hbm).wait_send()

    @pl.when(seam)
    def _():
        for r in range(PARTS // 2):
            from_relay(0, r).wait_send()

    for d in range(1, NZ):
        stat_z(d).wait_send()
    stat_y.wait_send()
    for k in (1, 2, 3):
        for view in (0, 1):
            stat_f(view, k).wait_send()
    for t in range(4):
        for s in range(HOPS):
            for copy in sum_send(t, s):
                copy.wait_send()
        y_copy(t).wait_send()
    hand1.wait_send()
    hand2.wait_send()
    hand3.wait_send()

    @pl.when(even)
    def _():
        hand6.wait_send()

    for lane in range(5):
        for s in range(HOPS):
            for copy in gather_send(lane, lane_tile[lane], s):
                copy.wait_send()
            if lane < 2:
                for i in (0, 1):
                    across(lane, lane_tile[lane], s, i).wait_send()
    for d in range(1, NZ):
        loss_z(d).wait_send()
    for r in range(4):
        loss_copy(r).wait_send()
    for view in (0, 1):
        for i in range(BANDS):
            out_copy(view, i).wait()


def local(view_a, view_b):
    rows, width = view_a.shape
    part = rows // PARTS
    band = rows // BANDS
    chunk = width // NZ
    dma = pltpu.SemaphoreType.DMA
    anywhere = pl.BlockSpec(memory_space=pl.ANY)
    grad_a, grad_b, loss = pl.pallas_call(
        kernel,
        out_shape=(
            jax.ShapeDtypeStruct((rows, width), F32),
            jax.ShapeDtypeStruct((rows, width), F32),
            jax.ShapeDtypeStruct((1, 1), F32),
        ),
        in_specs=[anywhere, anywhere],
        out_specs=(anywhere, anywhere, pl.BlockSpec(memory_space=pltpu.SMEM)),
        scratch_shapes=[
            pltpu.VMEM((4, rows, width), F32),
            pltpu.VMEM((4, rows, width), F32),
            pltpu.VMEM((BANDS + 1, width, band), BF16),
            pltpu.VMEM((BANDS + 1, width, band), BF16),
            pltpu.VMEM((band, width), BF16),
            pltpu.VMEM((band, width), BF16),
            pltpu.VMEM((4, width, width), F32),
            pltpu.VMEM((4, HOPS, chunk, width), F32),
            pltpu.VMEM((4, HOPS, chunk, width), F32),
            pltpu.VMEM((4, chunk, width), F32),
            pltpu.VMEM((chunk, width), F32),
            pltpu.VMEM((7, width, width), F32),
            pltpu.VMEM((width, width), BF16),
            pltpu.VMEM((width, width), BF16),
            pltpu.VMEM((rows, width), F32),
            pltpu.VMEM((rows, width), F32),
            pltpu.VMEM((PARTS // 2, part, width), F32),
            pltpu.VMEM((NZ, 8, width), F32),
            pltpu.VMEM((2, 8, width), F32),
            pltpu.VMEM((4, 8, width), F32),
            pltpu.VMEM((4, 8, width), F32),
            pltpu.VMEM((width, 128), F32),
            pltpu.VMEM((8, width), F32),
            pltpu.VMEM((2, 16, width), F32),
            pltpu.VMEM((NZ, 8, 128), F32),
            pltpu.VMEM((5, 8, 128), F32),
            pltpu.VMEM((4, 8, 128), F32),
            dma((2,)),
            dma((2, BANDS)),
            dma((2, PARTS)), dma((2, PARTS)),
            dma((2, PARTS)), dma((2, PARTS)),
            dma((2,)), dma((2,)),
            dma((PARTS // 2,)), dma((PARTS // 2,)),
            dma((NZ,)), dma((NZ,)),
            dma(()), dma(()),
            dma((2, 4)), dma((2, 4)),
            dma((2, 4, HOPS)), dma((2, 4, HOPS)),
            dma((4,)), dma((4,)),
            dma((4,)), dma((7,)),
            dma((2, 5, HOPS)), dma((2, 5, HOPS)),
            dma((2, 2, HOPS)), dma((2, 2, HOPS)),
            dma((NZ,)), dma((NZ,)),
            dma((4,)), dma((4,)),
        ],
        compiler_params=pltpu.CompilerParams(
            collective_id=0, has_side_effects=True, vmem_limit_bytes=60 * 1024 * 1024
        ),
        cost_estimate=pl.CostEstimate(
            flops=2 * 3 * 12 * rows * width * width, bytes_accessed=16 * rows * width, transcendentals=0
        ),
    )(view_a, view_b)
    return grad_a, grad_b, loss[0, 0]


def solution(mesh):
    spec = P("batch", "feat")
    return jax.shard_map(
        local, mesh=mesh, in_specs=(spec, spec), out_specs=(spec, spec, P()), check_vma=False
    )
```

time: 617 us -> 214 us (0.35)
  waiting for transfers between devices: 260 us -> 0 us
  blocking collectives: 229 us -> 0 us
  Pallas kernels: 0 us -> 203 us
  matrix products: 61 us -> 0 us
  other arithmetic: 18 us -> 0 us
  between operations: 20.1 us -> 2.47 us
  starting transfers between devices: 14.7 us -> 0 us
    psum x4 -> x0, blocking collectives: 229 us -> none  [the longest x1 128 us: local(): loss = lax.psum(local_loss, 'feat') / features]
    pallas_call x0 -> x1, Pallas kernels: none -> 203 us  [local(): pl.pallas_call(kernel, out_shape=(jax.ShapeDtypeStruct((rows, width), F32...]
    psum x1 -> x0, waiting for transfers between devices: 203 us -> none  [local(): lax.psum(cross_tile(norm_a, block), 'batch') / total]
    dot_general x12 -> x0, matrix products: 61 us -> none  [the longest x4 24.5 us: local(): jnp.dot(norm_a, weights[step], precision=highest)]
    ppermute x6 -> x0, waiting for transfers between devices: 56.8 us -> none  [from_behind(): return lax.ppermute(value, axis, pairs)]
    ppermute x6 -> x0, starting transfers between devices: 14.7 us -> none  [from_behind(): return lax.ppermute(value, axis, pairs)]
    reduce_sum x9 -> x0, other arithmetic: 10.6 us -> none  [the longest x4 5.71 us: local(): local_loss = local_loss + off_weight * jnp.sum(tile * tile)]
    gather x1 -> x0, local copies, waits for them, and re-layouts: 8.78 us -> none  [local(): diagonal = jnp.diagonal(tiles[0])]
  transfers between devices with their start and end apart: 7 -> 0, of which waited for: 4 -> 0; matrix products, arithmetic and copies ran while one was open for 7% -> 0% of each run, Pallas kernels for 0% -> 0%
where the time goes in v1:
time: 214 us; the launch traced here: 210 us
  Pallas kernels  203 us (95%)
  local copies, waits for them, and re-layouts  4.55 us (2%)
  between operations  2.47 us (1%)
    pallas_call x1, Pallas kernels, local(): pl.pallas_call(kernel, out_shape=(jax.ShapeDtypeStruct((rows, width), F32...  203 us
    unnamed x4, local copies, waits for them, and re-layouts  4.55 us

profile of v1, /device:TPU:16, one launch (start us, length us, event | category | flops | bytes accessed | tf_op | source)
XLA Modules:
  0.0 210.3 jit_solution(15920664453244683411)
XLA Ops:
  0.6 203.3 %shard_map.49 = (f32[1024,512]{1,0:T(8,128)}, f32[1024,512]{1,0:T(8,128)}, f32[1,1]{1,0:T(1,128)}) custom-call(f32[1024,512]{1,0:T(8,128)} %a_hbm.1, f32[1024,512]{1,0:T(8,128)} %b_hbm.1), custom_call_target="tpu_custom_call" | custom-call | flops 19327352832 | bytes 8388608 | tf_op jit(solution)/shard_map/pallas_call | solution.py:743
  203.9 0.0 copy-start
  203.9 3.2 %copy.8 = f32[1024,512]{1,0:T(8,128)} copy(f32[1024,512]{1,0:T(8,128)} %get-tuple-element.12) | data formatting | bytes 4194304
  207.1 0.0 copy-done
  207.2 1.3 copy.9
Async XLA Ops:
  203.9 3.2 %copy-start = (f32[1024,512]{1,0:T(8,128)S(1)}, f32[1024,512]{1,0:T(8,128)}, u32[]{:S(2)}) copy-start(f32[1024,512]{1,0:T(8,128)} %get-tuple-element.13) | copy-start | bytes 6291460

commit v2 on v1

v2 whole, which is shorter than its diff:
```python
import functools

import jax
import jax.numpy as jnp
from jax import lax
from jax.experimental import pallas as pl
from jax.experimental.pallas import tpu as pltpu
from jax.sharding import PartitionSpec as P

MESH = pl.DeviceIdType.MESH
F32 = jnp.float32
BF16 = jnp.bfloat16

eps = 1e-05
off_weight = 0.25

NZ = 8
NX = 4
NY = 4
NF = 16
PARTS = 8
BANDS = 4
HOPS = 4
AHEAD = 3

ORDER = (
    "OWN", "R0", "S0_0", "P0", "T3O", "C00", "S0_1", "S3o_0", "P1", "P2", "S0_2", "C01", "S3o_1",
    "R1", "C02", "S0_3", "S3o_2", "R2", "S0_4", "S3o_3", "P3", "P4", "F0", "G0_0", "S3o_4", "C03",
    "S10_0", "C10", "P5", "S20_0", "G0_1", "S10_1", "S20_1", "C11", "R3", "G0_2", "P6", "S10_2",
    "F3o", "S20_2", "GE_0", "C12", "G0_3", "P7", "LT0", "S10_3", "LT1", "S20_3", "GE_1", "C31",
    "C32", "C30", "RL0", "C33", "S3e_0", "S20_4", "GE_2", "S10_4", "C13", "S11_0", "S21_0", "S3e_1",
    "LT2", "LT3", "F20", "GE_3", "G0_4", "S11_1", "Wb0", "S21_1", "S3e_2", "F10", "GA0_0", "Wa0",
    "S21_2", "S3e_3", "S11_2", "RL1", "GE_4", "GA0_1", "S21_3", "WE", "GD0_0", "S11_3", "GA0_2",
    "S3e_4", "S21_4", "GC0_0", "GD0_1", "S11_4", "GA0_3", "GC0_1", "GD0_2", "F3e", "GA0_4", "F21",
    "GC0_2", "F11", "X0", "GA1_0", "GD0_3", "GC0_3", "X1", "GA1_1", "GD0_4", "GC0_4", "GL_0", "X2",
    "GA1_2", "X3", "X4", "GD1_0", "GL_1", "X5", "GA1_3", "GC1_0", "GD1_1", "GL_2", "GA1_4", "WA",
    "GC1_1", "GD1_2", "GL_3", "WO", "GC1_2", "GD1_3", "GL_4", "WL", "GD1_4", "GC1_3", "WD", "GC1_4",
    "WC", "END",
)


def mod(value, n):
    return lax.rem(value + n, n)


def split(value):
    hi = value.astype(BF16)
    return hi, (value - hi.astype(F32)).astype(BF16)


def dot3(left, right, transposed=False):
    dims = (((1,), (1 if transposed else 0,)), ((), ()))
    dot = functools.partial(lax.dot_general, dimension_numbers=dims, preferred_element_type=F32)
    return dot(left[0], right[0]) + dot(left[0], right[1]) + dot(left[1], right[0])


def kernel(
    a_hbm, b_hbm, ga_hbm, gb_hbm, loss_ref,
    raw_a, raw_b, at_hi, at_lo, b_hi, b_lo, tiles, rs_p, rs_m, y_recv, fin, cfull, c_hi, c_lo,
    g_a, g_b, relay_a, relay_b, relay_far, st_z, st_y, st_a, st_b, squares, columns, means, l_z, l_send, l_recv,
    in_sem, out_sem, direct_s, direct_r, fwd_s, fwd_r, far_s, far_r, rel_s, rel_r, rel_far_s, rel_far_r,
    stz_s, stz_r, sty_s, sty_r, stf_s, stf_r, rs_s, rs_r, y_s, y_r, hand_s, hand_r,
    ag_s, ag_r, ay_s, ay_r, ae_s, ae_r, lz_s, lz_r, loss_s, loss_r,
):
    rows, width = a_hbm.shape
    part = rows // PARTS
    band = rows // BANDS
    chunk = width // NZ
    half = chunk // 2
    total = float(rows * 2 * NZ)
    features = float(width * NF)

    batch = lax.axis_index("batch")
    feat = lax.axis_index("feat")
    z = lax.div(batch, 2)
    y_lo = lax.rem(batch, 2)
    y = lax.div(feat, 2 * NX) * 2 + y_lo
    x = lax.rem(lax.div(feat, 2), NX)
    core = lax.rem(feat, 2)
    even = core == 0
    odd = core == 1
    first_x = x == 0
    last_x = x == NX - 1
    seam = jnp.logical_or(first_x, last_x)

    def at_feat(f):
        return {"batch": batch, "feat": f}

    def at_z(z_other):
        return {"batch": z_other * 2 + y_lo, "feat": feat}

    def at_xy(x_other, y_other, core_other):
        f = lax.div(y_other, 2) * (2 * NX) + x_other * 2 + core_other
        return {"batch": z * 2 + lax.rem(y_other, 2), "feat": f}

    def neighbour(steps):
        return at_feat(mod(feat + steps, NF))

    def crossed(stride):
        return at_feat(feat + stride - 2 * stride * lax.rem(lax.div(feat, stride), 2))

    other_core = crossed(1)
    other_y = {"batch": batch + 1 - 2 * y_lo, "feat": feat}
    above = at_z(mod(z + 1, NZ))
    below = at_z(mod(z - 1, NZ))
    mirror_x = NX - 1 - x
    ahead_crossed = at_feat(mod(feat + 3 - 2 * core, NF))

    def send(src, dst, s_sem, r_sem, device):
        return pltpu.make_async_remote_copy(
            src_ref=src, dst_ref=dst, send_sem=s_sem, recv_sem=r_sem,
            device_id=device, device_id_type=MESH,
        )

    def landed(dst, r_sem, s_sem):
        send(dst, dst, s_sem, r_sem, other_core).wait_recv()

    load_b = pltpu.make_async_copy(b_hbm, raw_b.at[0], in_sem.at[0])
    load_a = pltpu.make_async_copy(a_hbm, raw_a.at[0], in_sem.at[1])
    load_b.start()
    load_a.start()

    barrier = pltpu.get_barrier_semaphore()
    friends = [neighbour(k) for k in (-3, -2, -1, 1, 2, 3)]
    friends += [crossed(k) for k in (2, 4, 8)]
    friends += [at_z(mod(z + d, NZ)) for d in range(1, NZ)]
    friends += [other_y]
    for friend in friends:
        pl.semaphore_signal(barrier, inc=1, device_id=friend, device_id_type=MESH)

    @pl.when(seam)
    def _():
        for friend in (
            at_xy(mirror_x, mod(y - 1, NY), core), at_xy(mirror_x, mod(y + 1, NY), core),
            at_xy(x, mod(y - 1, NY), core), at_xy(x, mod(y + 1, NY), core),
            at_xy(x, mod(y - 1, NY), 1 - core), at_xy(x, mod(y + 1, NY), 1 - core),
        ):
            pl.semaphore_signal(barrier, inc=1, device_id=friend, device_id_type=MESH)

    pl.semaphore_wait(barrier, jnp.where(seam, len(friends) + 6, len(friends)))


    def band_of(c):
        return pl.ds(pl.multiple_of(c * band, band), band)

    def span(i, size):
        return pl.ds(pl.multiple_of(i * size, size), size)

    halves = (pl.ds(0, width // 2), pl.ds(width // 2, width // 2))

    def piece(view, j):
        if view == 0:
            return span(j, part), pl.ds(0, width)
        return span(j % BANDS, band), halves[j // BANDS]

    raws = (raw_a, raw_b)
    relays = (relay_a, relay_b)

    def direct(view, j):
        src, raw, steps = ((a_hbm, raw_a, 2), (b_hbm, raw_b, -2))[view]
        return send(
            src.at[piece(view, j)], raw.at[1, *piece(view, j)], direct_s.at[view, j], direct_r.at[view, j],
            neighbour(steps),
        )

    def to_relay(view, j):
        src = (a_hbm, b_hbm)[view]
        return send(
            src.at[piece(view, j)], relays[view].at[j // 2], direct_s.at[view, j], rel_r.at[view, j // 2],
            at_xy(mirror_x, mod(y - 1, NY), core),
        )

    def from_relay(view, r):
        j = 2 * r + 1
        return send(
            relays[view].at[r], raws[view].at[1, *piece(view, j)], rel_s.at[view, r], direct_r.at[view, j],
            at_xy(x, mod(y - 1, NY), core),
        )

    leaves = (last_x, first_x)
    enters = (first_x, last_x)

    def when(cond, f, *args):
        @pl.when(cond)
        def _():
            f(*args)

    def piece_start(j):
        for view in (1, 0):
            if j % 2 == 0:
                direct(view, j).start()
            else:
                @pl.when(leaves[view])
                def _():
                    to_relay(view, j).start()

                @pl.when(jnp.logical_not(leaves[view]))
                def _():
                    direct(view, j).start()

    for j in range(AHEAD):
        piece_start(j)

    def far(view, j, src=None):
        raw = raws[view]
        src = raw.at[1] if src is None else src
        return send(
            src.at[band_of(j)], raw.at[3, band_of(j)], far_s.at[view, j], far_r.at[view, j],
            neighbour(1 - 2 * view),
        )

    def far_to_relay(view, j):
        return send(
            raws[view].at[1, band_of(j)], relay_far.at[j // 2], far_s.at[view, j], rel_far_r.at[j // 2],
            at_xy(mirror_x, mod(y - 1, NY), core),
        )

    def far_from_relay(view, r):
        j = 2 * r + 1
        return send(
            relay_far.at[r], raws[view].at[3, band_of(j)], rel_far_s.at[r], far_r.at[view, j],
            at_xy(x, mod(y - 1, NY), 1 - core),
        )

    for j in range(BANDS):
        when(odd, lambda: far(1, j, b_hbm).start())
        when(even, lambda: far(0, j, a_hbm).start())

    load_b.wait()
    load_a.wait()
    strip = 128
    for view, raw in ((0, raw_a), (1, raw_b)):
        def add_up(i, acc):
            v = raw[0, pl.ds(pl.multiple_of(i * strip, strip), strip), :]
            return acc + jnp.sum(v.reshape(strip // 8, 8, width), axis=0)

        zeros = jnp.zeros((8, width), F32)
        acc = lax.fori_loop(0, rows // strip, add_up, zeros)
        mean = jnp.sum(acc, axis=0, keepdims=True) * (1.0 / rows)

        def add_up_squares(i, carry):
            rest, square = carry
            v = raw[0, pl.ds(pl.multiple_of(i * strip, strip), strip), :] - mean
            v = v.reshape(strip // 8, 8, width)
            return rest + jnp.sum(v, axis=0), square + jnp.sum(v * v, axis=0)

        rest, square = lax.fori_loop(0, rows // strip, add_up_squares, (zeros, zeros))
        st_z[z, pl.ds(3 * view, 1), :] = mean
        st_z[z, pl.ds(3 * view + 1, 1), :] = jnp.sum(square, axis=0, keepdims=True)
        st_z[z, pl.ds(3 * view + 2, 1), :] = jnp.sum(rest, axis=0, keepdims=True)

    def stat_z(d):
        return send(
            st_z.at[z], st_z.at[z], stz_s.at[d], stz_r.at[d], at_z(mod(z + d, NZ))
        )

    for d in range(1, NZ):
        stat_z(d).start()
    for d in range(1, NZ):
        landed(st_z.at[mod(z - d, NZ)], stz_r.at[d], stz_s.at[d])
    for view in (0, 1):
        means_z = [st_z[i, pl.ds(3 * view, 1), :] for i in range(NZ)]
        mean = sum(means_z[1:], means_z[0]) * (1.0 / NZ)
        square = jnp.zeros((1, width), F32)
        rest = jnp.zeros((1, width), F32)
        for i in range(NZ):
            off = means_z[i] - mean
            square = square + (st_z[i, pl.ds(3 * view + 1, 1), :] + float(rows) * off * off)
            rest = rest + (st_z[i, pl.ds(3 * view + 2, 1), :] + float(rows) * off)
        st_y[0, pl.ds(3 * view, 1), :] = mean
        st_y[0, pl.ds(3 * view + 1, 1), :] = square
        st_y[0, pl.ds(3 * view + 2, 1), :] = rest
    stat_y = send(st_y.at[0], st_y.at[1], sty_s, sty_r, other_y)
    stat_y.start()
    stat_y.wait_recv()
    rows_z = float(rows * NZ)
    for view, st in ((0, st_a), (1, st_b)):
        mean0, mean1 = (st_y[i, pl.ds(3 * view, 1), :] for i in (0, 1))
        mean = 0.5 * (mean0 + mean1)
        off0, off1 = mean0 - mean, mean1 - mean
        square = (
            st_y[0, pl.ds(3 * view + 1, 1), :] + st_y[1, pl.ds(3 * view + 1, 1), :]
            + rows_z * (off0 * off0 + off1 * off1)
        )
        rest = (
            st_y[0, pl.ds(3 * view + 2, 1), :] + st_y[1, pl.ds(3 * view + 2, 1), :]
            + rows_z * (off0 + off1)
        )
        inverse = 1.0 / jnp.sqrt(square * (1.0 / total) + eps)
        st[0, pl.ds(0, 1), :] = mean
        st[0, pl.ds(1, 1), :] = inverse
        st[0, pl.ds(2, 1), :] = rest * (1.0 / total) * inverse

    def stat_f(view, k):
        st = (st_a, st_b)[view]
        if k == 2:
            slot = 1
        elif (k == 1) == (view == 1):
            slot = 2 + core
        else:
            slot = 3 - core
        return send(
            st.at[0], st.at[slot], stf_s.at[view, k], stf_r.at[view, slot],
            neighbour(-k if view == 1 else k),
        )

    for k in (2, 1, 3):
        for view in (1, 0):
            stat_f(view, k).start()

    def normal(raw, st, slot, rows_here, cols=slice(None)):
        return (raw[slot, rows_here, cols] - st[slot, pl.ds(0, 1), cols]) * st[slot, pl.ds(1, 1), cols]

    def products(c, store):
        def rows_of(i, carry):
            here = span(i, width // 2)
            store(here, dot3((at_hi[c, here, :], at_lo[c, here, :]), (b_hi[...], b_lo[...])))
            return carry
        lax.fori_loop(0, 2, rows_of, 0)

    def add_tile(t, c):
        def store(here, out):
            tiles[t, here, :] = tiles[t, here, :] + out
        products(c, store)

    def add_halves(h, c):
        cols, mid = halves[h], width // 2
        def store(here, out):
            tiles[1, here, cols] = tiles[1, here, cols] + out[:, :mid]
            tiles[2, here, cols] = tiles[2, here, cols] + out[:, mid:]
        products(c, store)

    def turn_a(slot, c, index):
        hi, lo = split(normal(raw_a, st_a, slot, band_of(c)).T)
        at_hi[index] = hi
        at_lo[index] = lo

    def take_b(slot, c):
        hi, lo = split(normal(raw_b, st_b, slot, band_of(c)))
        b_hi[...] = hi
        b_lo[...] = lo

    def take_halves(h, c):
        for slot in (1, 2):
            hi, lo = split(normal(raw_b, st_b, slot, band_of(c), halves[h]))
            b_hi[:, halves[slot - 1]] = hi
            b_lo[:, halves[slot - 1]] = lo

    def clear(t, carry):
        tiles[t] = jnp.zeros((width, width), F32)
        return carry

    lax.fori_loop(0, 4, clear, 0)

    def own_tile(c, carry):
        turn_a(0, c, c)
        take_b(0, c)
        add_tile(0, c)
        return carry

    def dest(q):
        return pl.multiple_of(mod(q, NZ) * chunk, chunk)

    whole = pl.ds(0, width)
    units = {"0": (0, whole), "3o": (3, whole), "3e": (3, whole)}
    for h in (0, 1):
        units["1%d" % h] = (1, halves[h])
        units["2%d" % h] = (2, halves[h])
    unit_sem = {"0": 0, "10": 1, "11": 2, "20": 3, "21": 4, "3o": 5, "3e": 5}

    def sum_send(unit, s):
        (t, cols), i = units[unit], unit_sem[unit]
        if s == 0:
            up = pl.ds(dest(z + HOPS), half)
            down = pl.ds(pl.multiple_of(dest(z + HOPS) + half, half), half)
            up_to, down_to = pl.ds(0, half), pl.ds(half, half)
        else:
            up, down = pl.ds(dest(z + HOPS - s), chunk), pl.ds(dest(z - HOPS + s), chunk)
            up_to = down_to = pl.ds(0, chunk)
        return (
            send(tiles.at[t, up, cols], rs_p.at[t, s, up_to, cols], rs_s.at[0, i, s], rs_r.at[0, i, s], above),
            send(tiles.at[t, down, cols], rs_m.at[t, s, down_to, cols], rs_s.at[1, i, s], rs_r.at[1, i, s], below),
        )

    def sum_start(unit, s):
        for copy in sum_send(unit, s):
            copy.start()

    def sum_take(unit, s):
        t, cols = units[unit]
        for copy in sum_send(unit, s):
            copy.wait_recv()
        for recv, q, low in ((rs_p, z + HOPS - 1 - s, 0), (rs_m, z - HOPS + 1 + s, half)):
            if s == 0:
                here = pl.ds(pl.multiple_of(dest(q) + low, half), half)
                tiles[t, here, cols] = tiles[t, here, cols] + recv[t, s, pl.ds(low, half), cols]
            else:
                here = pl.ds(dest(q), chunk)
                tiles[t, here, cols] = tiles[t, here, cols] + recv[t, s, :, cols]

    mine = pl.ds(dest(z), chunk)

    def y_copy(unit):
        (t, cols), i = units[unit], unit_sem[unit]
        return send(tiles.at[t, mine, cols], y_recv.at[t, :, cols], y_s.at[i], y_r.at[i], other_y)

    def sum_step(unit, s):
        if s > 0:
            sum_take(unit, s - 1)
        if s < HOPS:
            sum_start(unit, s)
        else:
            y_copy(unit).start()

    def sum_all(unit):
        t, cols = units[unit]
        y_copy(unit).wait_recv()
        return (tiles[t, mine, cols] + y_recv[t, :, cols]) * (1.0 / total)

    def hand(u, h=0):
        if u in (4, 5):
            src = cfull.at[u - 3, mine, halves[h]]
            dst = cfull.at[u, mine, halves[h]]
            device = neighbour(2) if u == 4 else ahead_crossed
        else:
            src, dst = fin, cfull.at[u, mine]
            device = neighbour(-1 if u == 3 else 2)
        return send(src, dst, hand_s.at[u, h], hand_r.at[u, h], device)

    def finish_sum(unit):
        value = sum_all(unit)
        t, cols = units[unit]
        if t < 3:
            cfull[t, mine, cols] = value
            if t > 0:
                hand(t + 3, int(unit[1])).start()
        else:
            fin[...] = value
            hand(3).start()
            if unit == "3o":
                cfull[6, mine, :] = value
            else:
                hand(6).start()

    def gather_part(s, mover):
        up, down = z - s - mover, z + s + mover
        if s < HOPS - 1:
            return pl.ds(dest(up), chunk), pl.ds(dest(down), chunk)
        return pl.ds(dest(up), half), pl.ds(pl.multiple_of(dest(down) + half, half), half)

    lanes = {"0": (0, 0, whole), "E": (1, 6, whole), "L": (2, 6 - 3 * core, whole)}
    for h in (0, 1):
        lanes["A%d" % h] = (3 + h, 1 + y_lo, halves[h])
        lanes["C%d" % h] = (5 + h, 4, halves[h])
        lanes["D%d" % h] = (7 + h, 5, halves[h])

    def gather_send(lane, s):
        i, u, cols = lanes[lane]
        up, down = gather_part(s, 0)
        return (
            send(cfull.at[u, up, cols], cfull.at[u, up, cols], ag_s.at[0, i, s], ag_r.at[0, i, s], above),
            send(cfull.at[u, down, cols], cfull.at[u, down, cols], ag_s.at[1, i, s], ag_r.at[1, i, s], below),
        )

    def across(lane, s, i):
        _, u, cols = lanes[lane]
        p = gather_part(s, 1)[i]
        if lane == "E":
            return send(cfull.at[6, p], cfull.at[3, p], ae_s.at[i, s], ae_r.at[i, s], other_core)
        h = int(lane[1])
        return send(
            cfull.at[u, p, cols], cfull.at[u, p, cols], ay_s.at[i, h, s], ay_r.at[i, h, s], other_y
        )

    def gather(lane, s):
        i, u, cols = lanes[lane]
        if s > 0:
            for d, p in enumerate(gather_part(s - 1, 1)):
                landed(cfull.at[u, p, cols], ag_r.at[d, i, s - 1], ag_s.at[d, i, s - 1])
                if lane[0] in "AE":
                    across(lane, s - 1, d).start()
        elif lane[0] in "CD":
            hand({"C": 4, "D": 5}[lane[0]], int(lane[1])).wait_recv()
        elif lane == "L":
            when(even, lambda: hand(6).wait_recv())
            when(odd, lambda: hand(3).wait_recv())
        if s < HOPS:
            for copy in gather_send(lane, s):
                copy.start()

    def gather_other(lane, u, cols):
        for s in range(HOPS):
            for i, p in enumerate(gather_part(s, 1)):
                if lane == "E":
                    landed(cfull.at[3, p], ae_r.at[i, s], ae_s.at[i, s])
                else:
                    h = int(lane[1])
                    landed(cfull.at[u, p, cols], ay_r.at[i, h, s], ay_s.at[i, h, s])

    def forward(view, j):
        raw = raws[view]
        return send(
            raw.at[1, *piece(view, j)], raw.at[2, *piece(view, j)], fwd_s.at[view, j], fwd_r.at[view, j],
            other_core,
        )

    def piece_take(j):
        for view in (1, 0):
            direct(view, j).wait_recv()
            forward(view, j).start()
        if j + AHEAD < PARTS:
            piece_start(j + AHEAD)

    def pass_on(r):
        for view in (1, 0):
            @pl.when(enters[view])
            def _():
                landed(relays[view].at[r], rel_r.at[view, r], rel_s.at[view, r])
                from_relay(view, r).start()

    def pass_far(r):
        for view, side in ((1, even), (0, odd)):
            @pl.when(jnp.logical_and(enters[view], side))
            def _():
                landed(relay_far.at[r], rel_far_r.at[r], rel_far_s.at[r])
                far_from_relay(view, r).start()

    def far_start(j):
        for view, side in ((1, even), (0, odd)):
            if j % 2 == 0:
                when(side, lambda: far(view, j).start())
            else:
                when(jnp.logical_and(side, leaves[view]), lambda: far_to_relay(view, j).start())
                when(
                    jnp.logical_and(side, jnp.logical_not(leaves[view])), lambda: far(view, j).start()
                )

    def far_take(view):
        for j in range(BANDS):
            far(view, j).wait_recv()

    def halves_step(h, c):
        forward(1, h * BANDS + c).wait_recv()
        take_halves(h, c)
        add_halves(h, c)

    def third_step(c):
        for j in (2 * c, 2 * c + 1):
            forward(0, j).wait_recv()

        @pl.when(even)
        def _():
            turn_a(2, c, BANDS)
            take_b(1, c)
            add_tile(3, BANDS)

    def fourth_tile():
        far_take(0)

        def body(c, carry):
            turn_a(3, c, BANDS)
            take_b(0, c)
            add_tile(3, BANDS)
            return carry

        lax.fori_loop(0, BANDS, body, 0)

    def grow(view, slot, u):
        g, raw, st = ((g_a, raw_b, st_b), (g_b, raw_a, st_a))[view]
        c = cfull[u]
        hi, lo = split(c)
        c_hi[...] = hi
        c_lo[...] = lo
        if view == 0:
            acc = squares[...]
            for j in range(width // 128):
                part_j = c[:, j * 128:(j + 1) * 128]
                acc = acc + part_j * part_j
            squares[...] = acc
        else:
            columns[...] = columns[...] + jnp.sum((c * c).reshape(width // 8, 8, width), axis=0)

        def body(i, carry):
            here = band_of(i)
            n = split(normal(raw, st, slot, here))
            g[here, :] = g[here, :] + dot3(n, (c_hi[...], c_lo[...]), view == 0)
            return carry

        lax.fori_loop(0, BANDS, body, 0)
        m = split(jnp.broadcast_to(st[slot, pl.ds(2, 1), :], (16, width)))
        means[view] = means[view] + dot3(m, (c_hi[...], c_lo[...]), view == 0)

    def grow_early():
        @pl.when(even)
        def _():
            far_take(1)
            hand(3).wait_recv()
            gather_other("E", 3, whole)
            grow(0, 3, 3)

        when(odd, grow, 1, 3, 6)

    def grow_late():
        @pl.when(odd)
        def _():
            far_take(1)
            grow(0, 3, 3)

        @pl.when(even)
        def _():
            far_take(0)
            grow(1, 3, 6)

    def grow_other():
        for h in (0, 1):
            gather_other("A%d" % h, 2 - y_lo, halves[h])
        grow(0, 2 - y_lo, 2 - y_lo)

    grows = {
        "a0": lambda: grow(0, 0, 0), "b0": lambda: grow(1, 0, 0),
        "A": lambda: grow(0, 1 + y_lo, 1 + y_lo), "O": grow_other,
        "C": lambda: grow(1, 1, 4), "D": lambda: grow(1, 2, 5),
        "E": grow_early, "L": grow_late,
    }

    def loss_part():
        value = jnp.zeros((8, 128), F32)
        for t in range(4):
            c = fin[...] if t == 3 else cfull[t, mine, :]
            terms = off_weight * c * c
            if t == 0:
                shape = (chunk, width)
                on = lax.broadcasted_iota(jnp.int32, shape, 1) == (
                    lax.broadcasted_iota(jnp.int32, shape, 0) + z * chunk
                )
                terms = jnp.where(on, (1.0 - c) * (1.0 - c), terms)
            terms = jnp.sum(terms.reshape(chunk // 8, 8, width), axis=0)
            for j in range(width // 128):
                value = value + terms[:, j * 128:(j + 1) * 128]
        l_z[z] = value

    def loss_z(d):
        return send(l_z.at[z], l_z.at[z], lz_s.at[d], lz_r.at[d], at_z(mod(z + d, NZ)))

    def loss_copy(r):
        return send(l_send.at[r], l_recv.at[r], loss_s.at[r], loss_r.at[r], crossed(1 << r))

    def loss_step(r):
        if r == 0:
            loss_part()
            for d in range(1, NZ):
                loss_z(d).start()
        elif r == 1:
            for d in range(1, NZ):
                landed(l_z.at[mod(z - d, NZ)], lz_r.at[d], lz_s.at[d])
            value = l_z[0]
            for i in range(1, NZ):
                value = value + l_z[i]
            l_send[0] = value
            loss_copy(0).start()
        else:
            loss_copy(r - 2).wait_recv()
            l_send[r - 1] = l_send[r - 2] + l_recv[r - 2]
            if r < 5:
                loss_copy(r - 1).start()

    squares[...] = jnp.zeros_like(squares)
    columns[...] = jnp.zeros_like(columns)
    means[...] = jnp.zeros_like(means)

    def clear_g(i, carry):
        g_a[band_of(i), :] = jnp.zeros((band, width), F32)
        g_b[band_of(i), :] = jnp.zeros((band, width), F32)
        return carry

    lax.fori_loop(0, BANDS, clear_g, 0)

    def step(name):
        kind, rest = name[0], name[1:]
        if name == "OWN":
            lax.fori_loop(0, BANDS, own_tile, 0)
            for slot in (3, 1, 2):
                for view, st in ((1, st_b), (0, st_a)):
                    landed(st.at[slot], stf_r.at[view, slot], stf_s.at[view, slot])
        elif name == "T3O":
            when(odd, fourth_tile)
        elif kind == "S":
            unit, s = rest.split("_")
            if unit[0] == "3":
                when(odd if unit == "3o" else even, sum_step, unit, int(s))
            else:
                sum_step(unit, int(s))
        elif kind == "F":
            if rest[0] == "3":
                when(odd if rest == "3o" else even, finish_sum, rest)
            else:
                finish_sum(rest)
        elif kind == "G":
            lane, s = rest.split("_")
            if lane == "E":
                when(odd, gather, lane, int(s))
            else:
                gather(lane, int(s))
        elif kind == "P":
            piece_take(int(rest))
        elif kind == "R":
            (pass_far if rest[0] == "L" else pass_on)(int(rest[-1]))
        elif kind == "C":
            if rest[0] == "3":
                third_step(int(rest[1]))
            else:
                halves_step(int(rest[0]), int(rest[1]))
        elif kind == "L":
            far_start(int(rest[1]))
        elif kind == "W":
            grows[rest]()
        elif kind == "X":
            loss_step(int(rest))

    for name in ORDER:
        step(name)

    loss_ref[0, 0] = jnp.sum(l_send[4]) * (1.0 / features)

    diagonal = []
    one_block = (
        lax.broadcasted_iota(jnp.int32, (128, 128), 0) == lax.broadcasted_iota(jnp.int32, (128, 128), 1)
    )
    for j in range(width // 128):
        block = cfull[0, j * 128:(j + 1) * 128, j * 128:(j + 1) * 128]
        diagonal.append(jnp.sum(jnp.where(one_block, block, 0.0), axis=0, keepdims=True))
    diagonal = jnp.concatenate(diagonal, axis=1)
    change = -(1.0 - diagonal) - off_weight * diagonal
    row_squares = jnp.sum(squares[...].T, axis=0, keepdims=True)
    column_squares = jnp.sum(columns[...], axis=0, keepdims=True)
    back_a = off_weight * row_squares + change * diagonal
    back_b = off_weight * column_squares + change * diagonal
    mean_a = off_weight * means[0, pl.ds(0, 1), :] + st_b[0, pl.ds(2, 1), :] * change
    mean_b = off_weight * means[1, pl.ds(0, 1), :] + st_a[0, pl.ds(2, 1), :] * change

    def out_copy(view, i):
        src, dst = ((g_a, ga_hbm), (g_b, gb_hbm))[view]
        return pltpu.make_async_copy(src.at[band_of(i)], dst.at[band_of(i)], out_sem.at[view, i])

    def finish(i, carry):
        here = band_of(i)
        n_a = normal(raw_a, st_a, 0, here)
        n_b = normal(raw_b, st_b, 0, here)
        g_a[here, :] = (off_weight * g_a[here, :] + n_b * change - mean_a - n_a * back_a) * st_a[0, pl.ds(1, 1), :]
        out_copy(0, i).start()
        g_b[here, :] = (off_weight * g_b[here, :] + n_a * change - mean_b - n_b * back_b) * st_b[0, pl.ds(1, 1), :]
        out_copy(1, i).start()
        return carry

    lax.fori_loop(0, BANDS, finish, 0)

    for view in (0, 1):
        for j in range(PARTS):
            direct(view, j).wait_send()
            forward(view, j).wait_send()
        for j in range(BANDS):
            far(view, j).wait_send()

        @pl.when(enters[view])
        def _():
            for r in range(PARTS // 2):
                from_relay(view, r).wait_send()

        @pl.when(jnp.logical_and(enters[view], (odd, even)[view]))
        def _():
            for r in range(BANDS // 2):
                far_from_relay(view, r).wait_send()

    for d in range(1, NZ):
        stat_z(d).wait_send()
        loss_z(d).wait_send()
    stat_y.wait_send()
    for k in (1, 2, 3):
        for view in (0, 1):
            stat_f(view, k).wait_send()
    for unit in ("0", "10", "11", "20", "21", "3o"):
        for s in range(HOPS):
            for copy in sum_send(unit, s):
                copy.wait_send()
        y_copy(unit).wait_send()
    for h in (0, 1):
        hand(4, h).wait_send()
        hand(5, h).wait_send()
    hand(3).wait_send()
    when(even, lambda: hand(6).wait_send())
    for lane in lanes:
        def sent(lane):
            for s in range(HOPS):
                for copy in gather_send(lane, s):
                    copy.wait_send()
                if lane[0] in "AE":
                    for i in (0, 1):
                        across(lane, s, i).wait_send()
        if lane == "E":
            when(odd, sent, lane)
        else:
            sent(lane)
    for r in range(4):
        loss_copy(r).wait_send()
    for view in (0, 1):
        for i in range(BANDS):
            out_copy(view, i).wait()


def local(view_a, view_b):
    rows, width = view_a.shape
    part = rows // PARTS
    band = rows // BANDS
    chunk = width // NZ
    dma = pltpu.SemaphoreType.DMA
    anywhere = pl.BlockSpec(memory_space=pl.ANY)
    grad_a, grad_b, loss = pl.pallas_call(
        kernel,
        out_shape=(
            jax.ShapeDtypeStruct((rows, width), F32),
            jax.ShapeDtypeStruct((rows, width), F32),
            jax.ShapeDtypeStruct((1, 1), F32),
        ),
        in_specs=[anywhere, anywhere],
        out_specs=(anywhere, anywhere, pl.BlockSpec(memory_space=pltpu.SMEM)),
        scratch_shapes=[
            pltpu.VMEM((4, rows, width), F32),
            pltpu.VMEM((4, rows, width), F32),
            pltpu.VMEM((BANDS + 1, width, band), BF16),
            pltpu.VMEM((BANDS + 1, width, band), BF16),
            pltpu.VMEM((band, width), BF16),
            pltpu.VMEM((band, width), BF16),
            pltpu.VMEM((4, width, width), F32),
            pltpu.VMEM((4, HOPS, chunk, width), F32),
            pltpu.VMEM((4, HOPS, chunk, width), F32),
            pltpu.VMEM((4, chunk, width), F32),
            pltpu.VMEM((chunk, width), F32),
            pltpu.VMEM((7, width, width), F32),
            pltpu.VMEM((width, width), BF16),
            pltpu.VMEM((width, width), BF16),
            pltpu.VMEM((rows, width), F32),
            pltpu.VMEM((rows, width), F32),
            pltpu.VMEM((PARTS // 2, part, width), F32),
            pltpu.VMEM((PARTS // 2, band, width // 2), F32),
            pltpu.VMEM((BANDS // 2, band, width), F32),
            pltpu.VMEM((NZ, 8, width), F32),
            pltpu.VMEM((2, 8, width), F32),
            pltpu.VMEM((4, 8, width), F32),
            pltpu.VMEM((4, 8, width), F32),
            pltpu.VMEM((width, 128), F32),
            pltpu.VMEM((8, width), F32),
            pltpu.VMEM((2, 16, width), F32),
            pltpu.VMEM((NZ, 8, 128), F32),
            pltpu.VMEM((5, 8, 128), F32),
            pltpu.VMEM((4, 8, 128), F32),
            dma((2,)),
            dma((2, BANDS)),
            dma((2, PARTS)), dma((2, PARTS)),
            dma((2, PARTS)), dma((2, PARTS)),
            dma((2, BANDS)), dma((2, BANDS)),
            dma((2, PARTS // 2)), dma((2, PARTS // 2)),
            dma((BANDS // 2,)), dma((BANDS // 2,)),
            dma((NZ,)), dma((NZ,)),
            dma(()), dma(()),
            dma((2, 4)), dma((2, 4)),
            dma((2, 6, HOPS)), dma((2, 6, HOPS)),
            dma((6,)), dma((6,)),
            dma((7, 2)), dma((7, 2)),
            dma((2, 9, HOPS)), dma((2, 9, HOPS)),
            dma((2, 2, HOPS)), dma((2, 2, HOPS)),
            dma((2, HOPS)), dma((2, HOPS)),
            dma((NZ,)), dma((NZ,)),
            dma((4,)), dma((4,)),
        ],
        compiler_params=pltpu.CompilerParams(
            collective_id=0, has_side_effects=True, vmem_limit_bytes=60 * 1024 * 1024
        ),
        cost_estimate=pl.CostEstimate(
            flops=2 * 3 * 12 * rows * width * width, bytes_accessed=16 * rows * width, transcendentals=0
        ),
    )(view_a, view_b)
    return grad_a, grad_b, loss[0, 0]


def solution(mesh):
    spec = P("batch", "feat")
    return jax.shard_map(
        local, mesh=mesh, in_specs=(spec, spec), out_specs=(spec, spec, P()), check_vma=False
    )
```

time: 214 us -> 221 us (1.033); the launches traced: 210 us -> 221 us
  Pallas kernels: 203 us -> 214 us
    pallas_call x1, Pallas kernels: 203 us -> 214 us  [local(): pl.pallas_call(kernel, out_shape=(jax.ShapeDtypeStruct((rows, width), F32...]
where the time goes in v2:
time: 221 us
  Pallas kernels  214 us (97%)
  local copies, waits for them, and re-layouts  4.55 us (2%)
  between operations  2.47 us (1%)
    pallas_call x1, Pallas kernels, local(): pl.pallas_call(kernel, out_shape=(jax.ShapeDtypeStruct((rows, width), F32...  214 us
    unnamed x4, local copies, waits for them, and re-layouts  4.55 us

profile of v2, /device:TPU:16, one launch (start us, length us, event | category | flops | bytes accessed | tf_op | source)
XLA Modules:
  0.0 220.9 jit_solution(10049463987630434074)
XLA Ops:
  0.6 213.9 %shard_map.49 = (f32[1024,512]{1,0:T(8,128)}, f32[1024,512]{1,0:T(8,128)}, f32[1,1]{1,0:T(1,128)}) custom-call(f32[1024,512]{1,0:T(8,128)} %a_hbm.1, f32[1024,512]{1,0:T(8,128)} %b_hbm.1), custom_call_target="tpu_custom_call" | custom-call | flops 19327352832 | bytes 8388608 | tf_op jit(solution)/shard_map/pallas_call | solution.py:817
  214.5 0.0 copy-start
  214.5 3.2 %copy.8 = f32[1024,512]{1,0:T(8,128)} copy(f32[1024,512]{1,0:T(8,128)} %get-tuple-element.12) | data formatting | bytes 4194304
  217.7 0.0 copy-done
  217.8 1.3 copy.9
Async XLA Ops:
  214.5 3.2 %copy-start = (f32[1024,512]{1,0:T(8,128)S(1)}, f32[1024,512]{1,0:T(8,128)}, u32[]{:S(2)}) copy-start(f32[1024,512]{1,0:T(8,128)} %get-tuple-element.13) | copy-start | bytes 6291460

commit v3 on v2

v3 whole, which is shorter than its diff:
```python
import functools

import jax
import jax.numpy as jnp
from jax import lax
from jax.experimental import pallas as pl
from jax.experimental.pallas import tpu as pltpu
from jax.sharding import PartitionSpec as P

MESH = pl.DeviceIdType.MESH
F32 = jnp.float32
BF16 = jnp.bfloat16

eps = 1e-05
off_weight = 0.25

NZ = 8
NX = 4
NY = 4
NF = 16
PARTS = 4
BANDS = 4
SLABS = 2
HOPS = 4
AHEAD = 3

ORDER = (
    "OWN", "R0", "S0_0", "T3O", "S3o_0", "S0_1", "P0", "S3o_1", "S0_2", "P1", "S3o_2", "C00",
    "S0_3", "S3o_3", "C01", "SH0_0", "S0_4", "R1", "S3o_4", "SH0_1", "P2", "SH0_2", "F0", "G0_0",
    "F3o", "GE_0", "C10", "P3", "LT0", "LT1", "SH0_3", "G0_1", "GE_1", "C11", "SH1_0", "C30",
    "SH1_1", "GE_2", "C31", "SH1_2", "S3e_0", "GE_3", "SH0_4", "RL0", "G0_2", "SH1_3", "S3e_1",
    "GE_4", "FH0", "GQ0_0", "WE", "G0_3", "SH1_4", "S3e_2", "GQ0_1", "GR0_0", "G0_4", "Wa", "Wb",
    "FH1", "GQ1_0", "S3e_3", "GQ0_2", "GR0_1", "GQ1_1", "GR1_0", "S3e_4", "GQ0_3", "F3e", "X0",
    "GR0_2", "GQ1_2", "GL_0", "X1", "GR1_1", "GQ0_4", "WQ0", "X2", "GR0_3", "X3", "GQ1_3", "X4",
    "GL_1", "X5", "GR1_2", "GR0_4", "WR0", "GQ1_4", "WQ1", "GL_2", "GR1_3", "GL_3", "GR1_4", "WR1",
    "GL_4", "WL", "END",
)


def mod(value, n):
    return lax.rem(value + n, n)


def split(value):
    hi = value.astype(BF16)
    return hi, (value - hi.astype(F32)).astype(BF16)


def dot(left, right):
    return lax.dot_general(left, right, (((1,), (0,)), ((), ())), preferred_element_type=F32)


def dot3(left_hi, left_lo, right_hi, right_lo):
    return dot(left_hi, right_hi) + dot(left_hi, right_lo) + dot(left_lo, right_hi)


def kernel(
    a_hbm, b_hbm, ra_hbm, rb_hbm, ct_hi_hbm, ct_lo_hbm, cb_hi_hbm, cb_lo_hbm, st_a, st_b, vectors, loss_ref,
    raw_a, raw_b, left_hi, left_lo, right_hi, right_lo, tiles, rs_p, rs_m, y_recv, fin, cfull,
    ct_hi, ct_lo, cb_hi, cb_lo, relay_a, relay_b, relay_far, st_z, st_y, squares, columns, means, l_z, l_send, l_recv,
    in_sem, block_sem, out_sem, direct_s, direct_r, fwd_s, fwd_r, far_s, far_r, rel_s, rel_r, rel_far_s, rel_far_r,
    stz_s, stz_r, sty_s, sty_r, stf_s, stf_r, rs_s, rs_r, y_s, y_r, hand_s, hand_r,
    ag_s, ag_r, ae_s, ae_r, lz_s, lz_r, loss_s, loss_r,
):
    rows, width = a_hbm.shape
    part = rows // PARTS
    band = rows // BANDS
    slab = rows // SLABS
    mid = width // 2
    chunk = width // NZ
    half = chunk // 2
    total = float(rows * 2 * NZ)
    features = float(width * NF)

    batch = lax.axis_index("batch")
    feat = lax.axis_index("feat")
    z = lax.div(batch, 2)
    y_lo = lax.rem(batch, 2)
    y = lax.div(feat, 2 * NX) * 2 + y_lo
    x = lax.rem(lax.div(feat, 2), NX)
    core = lax.rem(feat, 2)
    even = core == 0
    odd = core == 1
    first_x = x == 0
    last_x = x == NX - 1
    seam = jnp.logical_or(first_x, last_x)

    def at_feat(f):
        return {"batch": batch, "feat": f}

    def at_z(z_other):
        return {"batch": z_other * 2 + y_lo, "feat": feat}

    def at_xy(x_other, y_other, core_other):
        f = lax.div(y_other, 2) * (2 * NX) + x_other * 2 + core_other
        return {"batch": z * 2 + lax.rem(y_other, 2), "feat": f}

    def neighbour(steps):
        return at_feat(mod(feat + steps, NF))

    def crossed(stride):
        return at_feat(feat + stride - 2 * stride * lax.rem(lax.div(feat, stride), 2))

    other_core = crossed(1)
    other_y = {"batch": batch + 1 - 2 * y_lo, "feat": feat}
    above = at_z(mod(z + 1, NZ))
    below = at_z(mod(z - 1, NZ))
    mirror_x = NX - 1 - x
    ahead_crossed = at_feat(mod(feat + 3 - 2 * core, NF))

    def send(src, dst, s_sem, r_sem, device):
        return pltpu.make_async_remote_copy(
            src_ref=src, dst_ref=dst, send_sem=s_sem, recv_sem=r_sem,
            device_id=device, device_id_type=MESH,
        )

    def landed(dst, r_sem):
        send(dst, dst, sty_s, r_sem, other_core).wait_recv()

    def left_here(src, s_sem):
        send(src, src, s_sem, sty_r, other_core).wait_send()

    load_b = pltpu.make_async_copy(b_hbm, raw_b.at[0], in_sem.at[0])
    load_a = pltpu.make_async_copy(a_hbm, raw_a.at[0], in_sem.at[1])
    load_b.start()
    load_a.start()

    barrier = pltpu.get_barrier_semaphore()
    friends = [neighbour(k) for k in (-3, -2, -1, 1, 2, 3)]
    friends += [crossed(k) for k in (2, 4, 8)]
    friends += [at_z(mod(z + d, NZ)) for d in range(1, NZ)]
    friends += [other_y]
    for friend in friends:
        pl.semaphore_signal(barrier, inc=1, device_id=friend, device_id_type=MESH)

    @pl.when(seam)
    def _():
        for friend in (
            at_xy(mirror_x, mod(y - 1, NY), core), at_xy(mirror_x, mod(y + 1, NY), core),
            at_xy(x, mod(y - 1, NY), core), at_xy(x, mod(y + 1, NY), core),
            at_xy(x, mod(y - 1, NY), 1 - core), at_xy(x, mod(y + 1, NY), 1 - core),
        ):
            pl.semaphore_signal(barrier, inc=1, device_id=friend, device_id_type=MESH)

    pl.semaphore_wait(barrier, jnp.where(seam, len(friends) + 6, len(friends)))


    def band_of(c):
        return pl.ds(pl.multiple_of(c * band, band), band)

    def span(i, size):
        return pl.ds(pl.multiple_of(i * size, size), size)

    halves = (pl.ds(0, mid), pl.ds(mid, mid))

    def piece(view, j):
        if view == 0:
            return span(j, part), pl.ds(0, width)
        return span(j % SLABS, slab), halves[j // SLABS]

    raws = (raw_a, raw_b)
    relays = (relay_a, relay_b)

    def direct(view, j):
        src, raw, steps = ((a_hbm, raw_a, 2), (b_hbm, raw_b, -2))[view]
        return send(
            src.at[piece(view, j)], raw.at[1, *piece(view, j)], direct_s.at[view, j], direct_r.at[view, j],
            neighbour(steps),
        )

    def to_relay(view, j):
        src = (a_hbm, b_hbm)[view]
        return send(
            src.at[piece(view, j)], relays[view].at[j // 2], direct_s.at[view, j], rel_r.at[view, j // 2],
            at_xy(mirror_x, mod(y - 1, NY), core),
        )

    def from_relay(view, r):
        j = 2 * r + 1
        return send(
            relays[view].at[r], raws[view].at[1, *piece(view, j)], rel_s.at[view, r], direct_r.at[view, j],
            at_xy(x, mod(y - 1, NY), core),
        )

    leaves = (last_x, first_x)
    enters = (first_x, last_x)

    def when(cond, f, *args):
        @pl.when(cond)
        def _():
            f(*args)

    def piece_start(j):
        for view in (1, 0):
            if j % 2 == 0:
                direct(view, j).start()
            else:
                @pl.when(leaves[view])
                def _():
                    to_relay(view, j).start()

                @pl.when(jnp.logical_not(leaves[view]))
                def _():
                    direct(view, j).start()

    for j in range(AHEAD):
        piece_start(j)

    def far(view, j, src=None):
        raw = raws[view]
        src = raw.at[1] if src is None else src
        return send(
            src.at[span(j, slab)], raw.at[3, span(j, slab)], far_s.at[view, j], far_r.at[view, j],
            neighbour(1 - 2 * view),
        )

    def far_to_relay(view, j):
        return send(
            raws[view].at[1, span(j, slab)], relay_far.at[j // 2], far_s.at[view, j], rel_far_r.at[j // 2],
            at_xy(mirror_x, mod(y - 1, NY), core),
        )

    def far_from_relay(view, r):
        j = 2 * r + 1
        return send(
            relay_far.at[r], raws[view].at[3, span(j, slab)], rel_far_s.at[r], far_r.at[view, j],
            at_xy(x, mod(y - 1, NY), 1 - core),
        )

    for j in range(SLABS):
        when(odd, lambda: far(1, j, b_hbm).start())
        when(even, lambda: far(0, j, a_hbm).start())

    load_b.wait()
    load_a.wait()
    strip = 128
    for view, raw in ((0, raw_a), (1, raw_b)):
        def add_up(i, acc):
            v = raw[0, pl.ds(pl.multiple_of(i * strip, strip), strip), :]
            return acc + jnp.sum(v.reshape(strip // 8, 8, width), axis=0)

        zeros = jnp.zeros((8, width), F32)
        acc = lax.fori_loop(0, rows // strip, add_up, zeros)
        mean = jnp.sum(acc, axis=0, keepdims=True) * (1.0 / rows)

        def add_up_squares(i, carry):
            rest, square = carry
            v = raw[0, pl.ds(pl.multiple_of(i * strip, strip), strip), :] - mean
            v = v.reshape(strip // 8, 8, width)
            return rest + jnp.sum(v, axis=0), square + jnp.sum(v * v, axis=0)

        rest, square = lax.fori_loop(0, rows // strip, add_up_squares, (zeros, zeros))
        st_z[z, pl.ds(3 * view, 1), :] = mean
        st_z[z, pl.ds(3 * view + 1, 1), :] = jnp.sum(square, axis=0, keepdims=True)
        st_z[z, pl.ds(3 * view + 2, 1), :] = jnp.sum(rest, axis=0, keepdims=True)

    def stat_z(d):
        return send(
            st_z.at[z], st_z.at[z], stz_s, stz_r, at_z(mod(z + d, NZ))
        )

    for d in range(1, NZ):
        stat_z(d).start()
    landed(st_z.at[pl.ds(0, NZ - 1)], stz_r)
    for view in (0, 1):
        means_z = [st_z[i, pl.ds(3 * view, 1), :] for i in range(NZ)]
        mean = sum(means_z[1:], means_z[0]) * (1.0 / NZ)
        square = jnp.zeros((1, width), F32)
        rest = jnp.zeros((1, width), F32)
        for i in range(NZ):
            off = means_z[i] - mean
            square = square + (st_z[i, pl.ds(3 * view + 1, 1), :] + float(rows) * off * off)
            rest = rest + (st_z[i, pl.ds(3 * view + 2, 1), :] + float(rows) * off)
        st_y[0, pl.ds(3 * view, 1), :] = mean
        st_y[0, pl.ds(3 * view + 1, 1), :] = square
        st_y[0, pl.ds(3 * view + 2, 1), :] = rest
    stat_y = send(st_y.at[0], st_y.at[1], sty_s, sty_r, other_y)
    stat_y.start()
    stat_y.wait_recv()
    rows_z = float(rows * NZ)
    for view, st in ((0, st_a), (1, st_b)):
        mean0, mean1 = (st_y[i, pl.ds(3 * view, 1), :] for i in (0, 1))
        mean = 0.5 * (mean0 + mean1)
        off0, off1 = mean0 - mean, mean1 - mean
        square = (
            st_y[0, pl.ds(3 * view + 1, 1), :] + st_y[1, pl.ds(3 * view + 1, 1), :]
            + rows_z * (off0 * off0 + off1 * off1)
        )
        rest = (
            st_y[0, pl.ds(3 * view + 2, 1), :] + st_y[1, pl.ds(3 * view + 2, 1), :]
            + rows_z * (off0 + off1)
        )
        inverse = 1.0 / jnp.sqrt(square * (1.0 / total) + eps)
        st[0, pl.ds(0, 1), :] = mean
        st[0, pl.ds(1, 1), :] = inverse
        st[0, pl.ds(2, 1), :] = rest * (1.0 / total) * inverse

    def stat_f(view, k):
        st = (st_a, st_b)[view]
        if k == 2:
            slot = 1
        elif (k == 1) == (view == 1):
            slot = 2 + core
        else:
            slot = 3 - core
        return send(
            st.at[0], st.at[slot], stf_s.at[view], stf_r.at[view],
            neighbour(-k if view == 1 else k),
        )

    for k in (2, 1, 3):
        for view in (1, 0):
            stat_f(view, k).start()

    def normal(raw, st, slot, rows_here, cols=slice(None)):
        return (raw[slot, rows_here, cols] - st[slot, pl.ds(0, 1), cols]) * st[slot, pl.ds(1, 1), cols]

    strips = 128

    def turn_a(slot, c, index):
        def body(i, carry):
            here = pl.ds(pl.multiple_of(c * slab + i * strips, strips), strips)
            hi, lo = split(normal(raw_a, st_a, slot, here).T)
            cols = pl.ds(pl.multiple_of(i * strips, strips), strips)
            left_hi[index, :, cols] = hi
            left_lo[index, :, cols] = lo
            return carry
        lax.fori_loop(0, slab // strips, body, 0)

    def take_b(slot, c):
        def body(i, carry):
            here = pl.ds(pl.multiple_of(c * slab + i * strips, strips), strips)
            right_hi[span(i, strips), :], right_lo[span(i, strips), :] = split(normal(raw_b, st_b, slot, here))
            return carry
        lax.fori_loop(0, slab // strips, body, 0)

    def take_halves(h, c):
        def body(i, carry):
            here = pl.ds(pl.multiple_of(c * slab + i * strips, strips), strips)
            for slot in (1, 2):
                hi, lo = split(normal(raw_b, st_b, slot, here, halves[h]))
                right_hi[span(i, strips), halves[slot - 1]] = hi
                right_lo[span(i, strips), halves[slot - 1]] = lo
            return carry
        lax.fori_loop(0, slab // strips, body, 0)

    def add_tile(t, c, first):
        def body(i, carry):
            here = span(i, mid)
            out = dot3(left_hi[c, here, :], left_lo[c, here, :], right_hi[...], right_lo[...])
            tiles[t, here, :] = out if first else tiles[t, here, :] + out
            return carry
        lax.fori_loop(0, 2, body, 0)

    def own_tile():
        for c in range(SLABS):
            turn_a(0, c, c)
            take_b(0, c)
            add_tile(0, c, c == 0)

    def dest(q):
        return pl.multiple_of(mod(q, NZ) * chunk, chunk)

    units = {"0": 0, "H0": 1, "H1": 2, "3o": 3, "3e": 3}

    def sum_send(unit, s):
        t = units[unit]
        if s == 0:
            up = pl.ds(dest(z + HOPS), half)
            down = pl.ds(pl.multiple_of(dest(z + HOPS) + half, half), half)
            up_to, down_to = pl.ds(0, half), pl.ds(half, half)
        else:
            up, down = pl.ds(dest(z + HOPS - s), chunk), pl.ds(dest(z - HOPS + s), chunk)
            up_to = down_to = pl.ds(0, chunk)
        return (
            send(tiles.at[t, up], rs_p.at[t, s, up_to], rs_s.at[t], rs_r.at[t, s], above),
            send(tiles.at[t, down], rs_m.at[t, s, down_to], rs_s.at[t], rs_r.at[t, s], below),
        )

    def sum_start(unit, s):
        for copy in sum_send(unit, s):
            copy.start()

    def sum_take(unit, s):
        t = units[unit]
        landed(tiles.at[t, pl.ds(0, chunk if s == 0 else 2 * chunk)], rs_r.at[t, s])
        for recv, q, low in ((rs_p, z + HOPS - 1 - s, 0), (rs_m, z - HOPS + 1 + s, half)):
            if s == 0:
                here = pl.ds(pl.multiple_of(dest(q) + low, half), half)
                tiles[t, here, :] = tiles[t, here, :] + recv[t, s, pl.ds(low, half), :]
            else:
                here = pl.ds(dest(q), chunk)
                tiles[t, here, :] = tiles[t, here, :] + recv[t, s]

    mine = pl.ds(dest(z), chunk)

    def y_copy(unit):
        t = units[unit]
        return send(tiles.at[t, mine], y_recv.at[t], y_s.at[t], y_r.at[t], other_y)

    def sum_step(unit, s):
        if s > 0:
            sum_take(unit, s - 1)
        if s < HOPS:
            sum_start(unit, s)
        else:
            y_copy(unit).start()

    def sum_all(unit):
        t = units[unit]
        y_copy(unit).wait_recv()
        return (tiles[t, mine, :] + y_recv[t]) * (1.0 / total)

    def hand(u, h=0):
        if u in (4, 5):
            src = cfull.at[1 + h, mine, halves[u - 4]]
            dst = cfull.at[4 + h, mine, halves[u - 4]]
            device = neighbour(2) if u == 4 else ahead_crossed
        else:
            src, dst = fin, cfull.at[u, mine]
            device = neighbour(-1 if u == 3 else 2)
        return send(src, dst, hand_s.at[u, h], hand_r.at[u, h], device)

    def finish_sum(unit):
        value = sum_all(unit)
        t = units[unit]
        if t < 3:
            cfull[t, mine, :] = value
            if t > 0:
                hand(4, t - 1).start()
                hand(5, t - 1).start()
        else:
            fin[...] = value
            hand(3).start()
            if unit == "3o":
                cfull[6, mine, :] = value
            else:
                hand(6).start()

    def gather_part(s, mover):
        up, down = z - s - mover, z + s + mover
        if s < HOPS - 1:
            return pl.ds(dest(up), chunk), pl.ds(dest(down), chunk)
        return pl.ds(dest(up), half), pl.ds(pl.multiple_of(dest(down) + half, half), half)

    lanes = {
        "0": (0, 0), "E": (1, 6), "L": (2, 6 - 3 * core),
        "Q0": (3, 1), "Q1": (4, 2), "R0": (5, 4), "R1": (6, 5),
    }

    def gather_send(lane, s):
        i, u = lanes[lane]
        return [
            send(cfull.at[u, p], cfull.at[u, p], ag_s.at[i], ag_r.at[i, s], device)
            for p, device in zip(gather_part(s, 0), (above, below))
        ]

    def across(s):
        return [
            send(cfull.at[6, p], cfull.at[3, p], ae_s, ae_r, other_core) for p in gather_part(s, 1)
        ]

    def gather(lane, s):
        i, u = lanes[lane]
        if s > 0:
            landed(cfull.at[u, pl.ds(0, 2 * chunk if s < HOPS else chunk)], ag_r.at[i, s - 1])
        elif lane[0] == "R":
            hand(4, int(lane[1])).wait_recv()
            hand(5, int(lane[1])).wait_recv()
        elif lane == "L":
            when(even, lambda: hand(6).wait_recv())
            when(odd, lambda: hand(3).wait_recv())
        if s < HOPS:
            for copy in gather_send(lane, s):
                copy.start()
        if s > 0 and lane == "E":
            for copy in across(s - 1):
                copy.start()

    def forward(view, j):
        raw = raws[view]
        return send(
            raw.at[1, *piece(view, j)], raw.at[2, *piece(view, j)], fwd_s.at[view, j], fwd_r.at[view, j],
            other_core,
        )

    def piece_take(j):
        for view in (1, 0):
            direct(view, j).wait_recv()
            forward(view, j).start()
        if j + AHEAD < PARTS:
            piece_start(j + AHEAD)

    def pass_on(r):
        for view in (1, 0):
            @pl.when(enters[view])
            def _():
                landed(relays[view].at[r], rel_r.at[view, r])
                from_relay(view, r).start()

    def pass_far(r):
        for view, side in ((1, even), (0, odd)):
            @pl.when(jnp.logical_and(enters[view], side))
            def _():
                landed(relay_far.at[r], rel_far_r.at[r])
                far_from_relay(view, r).start()

    def far_start(j):
        for view, side in ((1, even), (0, odd)):
            if j % 2 == 0:
                when(side, lambda: far(view, j).start())
            else:
                when(jnp.logical_and(side, leaves[view]), lambda: far_to_relay(view, j).start())
                when(
                    jnp.logical_and(side, jnp.logical_not(leaves[view])), lambda: far(view, j).start()
                )

    def far_take(view):
        for j in range(SLABS):
            far(view, j).wait_recv()

    def halves_step(h, c):
        forward(1, h * SLABS + c).wait_recv()
        take_halves(h, c)
        add_tile(1 + h, c, c == 0)

    def third_step(c):
        for j in range(c * SLABS, c * SLABS + SLABS):
            forward(0, j).wait_recv()

        @pl.when(even)
        def _():
            turn_a(2, c, SLABS)
            take_b(1, c)
            add_tile(3, SLABS, c == 0)

    def fourth_tile():
        far_take(0)
        for c in range(SLABS):
            turn_a(3, c, SLABS)
            take_b(0, c)
            add_tile(3, SLABS, c == 0)

    def block_out(view, slot):
        raw, dst = ((raw_a, ra_hbm), (raw_b, rb_hbm))[view]
        return pltpu.make_async_copy(raw.at[slot], dst.at[slot - 1], block_sem.at[view, slot - 1])

    def tile_out(view, k, cols=slice(None), count=1, i=0):
        here = pl.ds(k * width, count * width)
        pairs = (((ct_hi, ct_hi_hbm), (ct_lo, ct_lo_hbm)), ((cb_hi, cb_hi_hbm), (cb_lo, cb_lo_hbm)))[view]
        return [
            pltpu.make_async_copy(src.at[here, cols], dst.at[here, cols], out_sem.at[view, k + i, j])
            for j, (src, dst) in enumerate(pairs)
        ]

    def keep(view, st, slot, at, to, cols, value):
        sums, hi_ref, lo_ref = ((squares, ct_hi, ct_lo), (columns, cb_hi, cb_lo))[view]
        sums[:, cols] = sums[:, cols] + jnp.sum((value * value).reshape(strips // 8, 8, -1), axis=0)
        factor = st[slot, :, pl.ds(at, strips)].T[:, 2:3]
        means[view, :, cols] = means[view, :, cols] + jnp.sum(
            (value * factor).reshape(strips // 8, 8, -1), axis=0
        )
        hi, lo = split(value)
        hi_ref[pl.ds(to, strips), cols] = hi
        lo_ref[pl.ds(to, strips), cols] = lo

    everything = slice(None)

    def keep_a(u, k, slots):
        for i in range(width // strips):
            value = cfull[u, :, pl.ds(i * strips, strips)].T
            slot, at = slots(i)
            keep(0, st_b, slot, at, k * width + i * strips, everything, value)
        for copy in tile_out(0, k):
            copy.start()

    def keep_b(u, k, slot):
        for i in range(width // strips):
            value = cfull[u, pl.ds(i * strips, strips), :]
            keep(1, st_a, slot, i * strips, k * width + i * strips, everything, value)
        for copy in tile_out(1, k):
            copy.start()

    def keep_a_half(h):
        per = mid // strips
        keep_a(1 + h, 1 + h, lambda i: (1 + i // per, h * mid + (i % per) * strips))

    def keep_b_half(h):
        for k in (1, 2):
            for i in range(width // strips):
                value = cfull[4 + h, pl.ds(i * strips, strips), halves[k - 1]]
                keep(1, st_a, k, i * strips, k * width + i * strips, halves[h], value)
        for copy in tile_out(1, 1, halves[h], 2, h):
            copy.start()

    def keep_early():
        @pl.when(even)
        def _():
            hand(3).wait_recv()
            landed(cfull.at[3, pl.ds(0, width - chunk)], ae_r)
            keep_a(3, 3, lambda i: (3, i * strips))

        when(odd, keep_b, 6, 3, 3)

    def keep_late():
        @pl.when(odd)
        def _():
            far_take(1)
            block_out(1, 3).start()
            keep_a(3, 3, lambda i: (3, i * strips))

        @pl.when(even)
        def _():
            far_take(0)
            block_out(0, 3).start()
            keep_b(6, 3, 3)

    keeps = {
        "a": lambda: keep_a(0, 0, lambda i: (0, i * strips)), "b": lambda: keep_b(0, 0, 0),
        "Q0": lambda: keep_a_half(0), "Q1": lambda: keep_a_half(1),
        "R0": lambda: keep_b_half(0), "R1": lambda: keep_b_half(1),
        "E": keep_early, "L": keep_late,
    }

    def blocks_out():
        for view in (0, 1):
            for slot in (1, 2):
                block_out(view, slot).start()

        @pl.when(even)
        def _():
            far_take(1)
            block_out(1, 3).start()

        when(odd, lambda: block_out(0, 3).start())

    def loss_part():
        value = jnp.zeros((8, 128), F32)
        for t in range(4):
            c = fin[...] if t == 3 else cfull[t, mine, :]
            terms = off_weight * c * c
            if t == 0:
                shape = (chunk, width)
                on = lax.broadcasted_iota(jnp.int32, shape, 1) == (
                    lax.broadcasted_iota(jnp.int32, shape, 0) + z * chunk
                )
                terms = jnp.where(on, (1.0 - c) * (1.0 - c), terms)
            terms = jnp.sum(terms.reshape(chunk // 8, 8, width), axis=0)
            for j in range(width // 128):
                value = value + terms[:, j * 128:(j + 1) * 128]
        l_z[z] = value

    def loss_z(d):
        return send(l_z.at[z], l_z.at[z], lz_s, lz_r, at_z(mod(z + d, NZ)))

    def loss_copy(r):
        return send(l_send.at[r], l_recv.at[r], loss_s.at[r], loss_r.at[r], crossed(1 << r))

    def loss_step(r):
        if r == 0:
            blocks_out()
            loss_part()
            for d in range(1, NZ):
                loss_z(d).start()
        elif r == 1:
            landed(l_z.at[pl.ds(0, NZ - 1)], lz_r)
            value = l_z[0]
            for i in range(1, NZ):
                value = value + l_z[i]
            l_send[0] = value
            loss_copy(0).start()
        else:
            loss_copy(r - 2).wait_recv()
            l_send[r - 1] = l_send[r - 2] + l_recv[r - 2]
            if r < 5:
                loss_copy(r - 1).start()

    squares[...] = jnp.zeros_like(squares)
    columns[...] = jnp.zeros_like(columns)
    means[...] = jnp.zeros_like(means)

    def step(name):
        kind, rest = name[0], name[1:]
        if name == "OWN":
            own_tile()
            for view, st in ((1, st_b), (0, st_a)):
                landed(st.at[pl.ds(1, 3)], stf_r.at[view])
        elif name == "T3O":
            when(odd, fourth_tile)
        elif kind == "S":
            unit, s = rest.split("_")
            if unit[0] == "3":
                when(odd if unit == "3o" else even, sum_step, unit, int(s))
            else:
                sum_step(unit, int(s))
        elif kind == "F":
            if rest[0] == "3":
                when(odd if rest == "3o" else even, finish_sum, rest)
            else:
                finish_sum(rest)
        elif kind == "G":
            lane, s = rest.split("_")
            if lane == "E":
                when(odd, gather, lane, int(s))
            else:
                gather(lane, int(s))
        elif kind == "P":
            piece_take(int(rest))
        elif kind == "R":
            (pass_far if rest[0] == "L" else pass_on)(int(rest[-1]))
        elif kind == "C":
            if rest[0] == "3":
                third_step(int(rest[1]))
            else:
                halves_step(int(rest[0]), int(rest[1]))
        elif kind == "L":
            far_start(int(rest[1]))
        elif kind == "W":
            keeps[rest]()
        elif kind == "X":
            loss_step(int(rest))

    for name in ORDER:
        step(name)

    loss_ref[0, 0] = jnp.sum(l_send[4]) * (1.0 / features)

    diagonal = []
    one_block = (
        lax.broadcasted_iota(jnp.int32, (128, 128), 0) == lax.broadcasted_iota(jnp.int32, (128, 128), 1)
    )
    for j in range(width // 128):
        block = cfull[0, j * 128:(j + 1) * 128, j * 128:(j + 1) * 128]
        diagonal.append(jnp.sum(jnp.where(one_block, block, 0.0), axis=0, keepdims=True))
    diagonal = jnp.concatenate(diagonal, axis=1)
    change = -(1.0 - diagonal) - off_weight * diagonal
    row_squares = jnp.sum(squares[...], axis=0, keepdims=True)
    column_squares = jnp.sum(columns[...], axis=0, keepdims=True)
    back_a = off_weight * row_squares + change * diagonal
    back_b = off_weight * column_squares + change * diagonal
    mean_a = off_weight * jnp.sum(means[0], axis=0, keepdims=True) + st_b[0, pl.ds(2, 1), :] * change
    mean_b = off_weight * jnp.sum(means[1], axis=0, keepdims=True) + st_a[0, pl.ds(2, 1), :] * change
    for i, row in enumerate((change, back_a, back_b, mean_a, mean_b)):
        vectors[pl.ds(i, 1), :] = row

    for view in (0, 1):
        for j in range(PARTS):
            direct(view, j).wait_send()
            forward(view, j).wait_send()
        for j in range(SLABS):
            far(view, j).wait_send()

        @pl.when(enters[view])
        def _():
            for r in range(PARTS // 2):
                from_relay(view, r).wait_send()

        @pl.when(jnp.logical_and(enters[view], (odd, even)[view]))
        def _():
            for r in range(SLABS // 2):
                far_from_relay(view, r).wait_send()

    left_here(st_z.at[pl.ds(0, NZ - 1)], stz_s)
    left_here(l_z.at[pl.ds(0, NZ - 1)], lz_s)
    stat_y.wait_send()
    for view, st in ((1, st_b), (0, st_a)):
        left_here(st.at[pl.ds(1, 3)], stf_s.at[view])
    for unit in ("0", "H0", "H1", "3o"):
        left_here(tiles.at[units[unit], pl.ds(0, width - chunk)], rs_s.at[units[unit]])
        y_copy(unit).wait_send()
    for h in (0, 1):
        hand(4, h).wait_send()
        hand(5, h).wait_send()
    hand(3).wait_send()
    when(even, lambda: hand(6).wait_send())
    for lane in lanes:
        i, u = lanes[lane]
        if lane == "E":
            @pl.when(odd)
            def _():
                left_here(cfull.at[6, pl.ds(0, width - chunk)], ag_s.at[1])
                left_here(cfull.at[6, pl.ds(0, width - chunk)], ae_s)
        else:
            left_here(cfull.at[u, pl.ds(0, width - chunk)], ag_s.at[i])
    for r in range(4):
        loss_copy(r).wait_send()
    for view in (0, 1):
        for slot in (1, 2, 3):
            block_out(view, slot).wait()
    for k in range(4):
        for copy in tile_out(0, k):
            copy.wait()
    for k in (0, 3):
        for copy in tile_out(1, k):
            copy.wait()
    for h in (0, 1):
        for copy in tile_out(1, 1, halves[h], 2, h):
            copy.wait()


def gradients(
    a_ref, b_ref, ra_ref, rb_ref, ct_hi, ct_lo, cb_hi, cb_lo, st_a, st_b, vectors, ga_ref, gb_ref, n_hi, n_lo
):
    width = a_ref.shape[1]
    mid = width // 2
    lower, upper = pl.ds(0, mid), pl.ds(mid, mid)

    def row(i):
        return vectors[pl.ds(i, 1), :]

    def normal(value, st, slot, cols=slice(None)):
        return (value - st[slot, pl.ds(0, 1), cols]) * st[slot, pl.ds(1, 1), cols]

    def put(at, value):
        hi, lo = split(value)
        n_hi[:, pl.ds(at, value.shape[1])] = hi
        n_lo[:, pl.ds(at, value.shape[1])] = lo

    change = row(0)
    norm_a = normal(a_ref[...], st_a, 0)
    norm_b = normal(b_ref[...], st_b, 0)
    put(0, norm_b)
    for h, cols in enumerate((lower, upper)):
        for slot in (1, 2):
            at = (1 + h) * width + (slot - 1) * mid
            put(at, normal(rb_ref[slot - 1, :, cols], st_b, slot, cols))
    put(3 * width, normal(rb_ref[2], st_b, 3))
    g = off_weight * dot3(n_hi[...], n_lo[...], ct_hi[...], ct_lo[...]) + norm_b * change
    ga_ref[...] = (g - row(3) - norm_a * row(1)) * st_a[0, pl.ds(1, 1), :]
    put(0, norm_a)
    for slot in (1, 2, 3):
        put(slot * width, normal(ra_ref[slot - 1], st_a, slot))
    g = off_weight * dot3(n_hi[...], n_lo[...], cb_hi[...], cb_lo[...]) + norm_a * change
    gb_ref[...] = (g - row(4) - norm_b * row(2)) * st_b[0, pl.ds(1, 1), :]


def local(view_a, view_b):
    rows, width = view_a.shape
    part = rows // PARTS
    band = rows // BANDS
    slab = rows // SLABS
    chunk = width // NZ
    dma = pltpu.SemaphoreType.DMA
    anywhere = pl.BlockSpec(memory_space=pl.ANY)
    in_vmem = pl.BlockSpec(memory_space=pltpu.VMEM)
    blocks = jax.ShapeDtypeStruct((3, rows, width), F32)
    sides = jax.ShapeDtypeStruct((BANDS * width, width), BF16)
    stats = jax.ShapeDtypeStruct((4, 8, width), F32)
    ra, rb, ct_hi, ct_lo, cb_hi, cb_lo, st_a, st_b, vectors, loss = pl.pallas_call(
        kernel,
        out_shape=(
            blocks, blocks, sides, sides, sides, sides, stats, stats,
            jax.ShapeDtypeStruct((8, width), F32), jax.ShapeDtypeStruct((1, 1), F32),
        ),
        in_specs=[anywhere, anywhere],
        out_specs=(anywhere,) * 6 + (in_vmem,) * 3 + (pl.BlockSpec(memory_space=pltpu.SMEM),),
        scratch_shapes=[
            pltpu.VMEM((4, rows, width), F32),
            pltpu.VMEM((4, rows, width), F32),
            pltpu.VMEM((SLABS + 1, width, slab), BF16),
            pltpu.VMEM((SLABS + 1, width, slab), BF16),
            pltpu.VMEM((slab, width), BF16),
            pltpu.VMEM((slab, width), BF16),
            pltpu.VMEM((4, width, width), F32),
            pltpu.VMEM((4, HOPS, chunk, width), F32),
            pltpu.VMEM((4, HOPS, chunk, width), F32),
            pltpu.VMEM((4, chunk, width), F32),
            pltpu.VMEM((chunk, width), F32),
            pltpu.VMEM((7, width, width), F32),
            pltpu.VMEM((4 * width, width), BF16),
            pltpu.VMEM((4 * width, width), BF16),
            pltpu.VMEM((4 * width, width), BF16),
            pltpu.VMEM((4 * width, width), BF16),
            pltpu.VMEM((PARTS // 2, part, width), F32),
            pltpu.VMEM((PARTS // 2, slab, width // 2), F32),
            pltpu.VMEM((SLABS // 2, slab, width), F32),
            pltpu.VMEM((NZ, 8, width), F32),
            pltpu.VMEM((2, 8, width), F32),
            pltpu.VMEM((8, width), F32),
            pltpu.VMEM((8, width), F32),
            pltpu.VMEM((2, 8, width), F32),
            pltpu.VMEM((NZ, 8, 128), F32),
            pltpu.VMEM((5, 8, 128), F32),
            pltpu.VMEM((4, 8, 128), F32),
            dma((2,)),
            dma((2, 3)),
            dma((2, 4, 2)),
            dma((2, PARTS)), dma((2, PARTS)),
            dma((2, PARTS)), dma((2, PARTS)),
            dma((2, SLABS)), dma((2, SLABS)),
            dma((2, PARTS // 2)), dma((2, PARTS // 2)),
            dma((SLABS // 2,)), dma((SLABS // 2,)),
            dma(()), dma(()),
            dma(()), dma(()),
            dma((2,)), dma((2,)),
            dma((4,)), dma((4, HOPS)),
            dma((4,)), dma((4,)),
            dma((7, 2)), dma((7, 2)),
            dma((7,)), dma((7, HOPS)),
            dma(()), dma(()),
            dma(()), dma(()),
            dma((4,)), dma((4,)),
        ],
        compiler_params=pltpu.CompilerParams(
            collective_id=0, has_side_effects=True, vmem_limit_bytes=60 * 1024 * 1024
        ),
        cost_estimate=pl.CostEstimate(
            flops=2 * 3 * 4 * rows * width * width, bytes_accessed=32 * rows * width, transcendentals=0
        ),
    )(view_a, view_b)

    def rows_of(*shape):
        return pl.BlockSpec(shape, lambda i: (0,) * (len(shape) - 2) + (i, 0))

    def once(*shape):
        return pl.BlockSpec(shape, lambda i: (0,) * len(shape), pipeline_mode=pl.Buffered(1))

    grad_a, grad_b = pl.pallas_call(
        gradients,
        grid=(BANDS,),
        out_shape=(jax.ShapeDtypeStruct((rows, width), F32),) * 2,
        in_specs=[rows_of(band, width)] * 2 + [rows_of(3, band, width)] * 2
        + [once(BANDS * width, width)] * 4 + [once(4, 8, width)] * 2 + [once(8, width)],
        out_specs=(rows_of(band, width),) * 2,
        scratch_shapes=[pltpu.VMEM((band, 4 * width), BF16), pltpu.VMEM((band, 4 * width), BF16)],
        compiler_params=pltpu.CompilerParams(vmem_limit_bytes=48 * 1024 * 1024),
        cost_estimate=pl.CostEstimate(
            flops=2 * 3 * 8 * rows * width * width, bytes_accessed=56 * rows * width, transcendentals=0
        ),
    )(view_a, view_b, ra, rb, ct_hi, ct_lo, cb_hi, cb_lo, st_a, st_b, vectors)
    return grad_a, grad_b, loss[0, 0]


def solution(mesh):
    spec = P("batch", "feat")
    return jax.shard_map(
        local, mesh=mesh, in_specs=(spec, spec), out_specs=(spec, spec, P()), check_vma=False
    )
```

time: 221 us -> 240 us (1.086)
  Pallas kernels: 214 us -> 232 us
    pallas_call x1 -> x2, Pallas kernels: 214 us -> 232 us  [the longest x1 213 us: local(): pl.pallas_call(kernel, out_shape=(blocks, blocks, sides, sides, sides, si...]
where the time goes in v3:
time: 240 us; the launch traced here: 239 us
  Pallas kernels  232 us (97%)
  local copies, waits for them, and re-layouts  3.99 us (2%)
  between operations  2.48 us (1%)
    pallas_call x1, Pallas kernels, local(): pl.pallas_call(kernel, out_shape=(blocks, blocks, sides, sides, sides, si...  213 us
    pallas_call x1, Pallas kernels, local(): pl.pallas_call(gradients, grid=(BANDS,), out_shape=(jax.ShapeDtypeStruct(...  19.4 us

profile of v3, /device:TPU:16, one launch (start us, length us, event | category | flops | bytes accessed | tf_op | source)
XLA Modules:
  0.0 238.5 jit_solution(581678413193887757)
XLA Ops:
  0.6 0.0 copy-start
  0.6 212.6 %shard_map.49 = (f32[3,1024,512]{2,1,0:T(8,128)}, f32[3,1024,512]{2,1,0:T(8,128)}, bf16[2048,512]{1,0:T(8,128)(2,1)}, bf16[2048,512]{1,0:T(8,128)(2,1)}, bf16[20...) custom-call(f32[1024,512]{1,0:T(8,128)} %a_ref.1, ...), custom_call_target="tpu_custom_call" | custom-call | flops 6442450944 | bytes 16777216 | tf_op jit(solution)/shard_map/pallas_call | solution.py:849
  213.3 0.0 copy-done
  213.3 0.0 copy-start.1
  213.3 1.6 copy-done.1
  214.9 0.0 copy-start.2
  214.9 0.8 copy-done.2
  215.7 0.0 copy-start.3
  215.7 0.8 copy-done.3
  216.6 0.0 copy-start.4
  216.6 0.7 copy-done.4
  217.3 19.4 %shard_map.50 = (f32[1024,512]{1,0:T(8,128)}, f32[1024,512]{1,0:T(8,128)}) custom-call(f32[1024,512]{1,0:T(8,128)S(1)} %copy-done, f32[1024,512]{1,0:T(8,128)S(1)} %copy-done.1, f32[3,1024,512]{2,1,0:T(8,128)} %get-tuple-element.15.ra_ref, f32[3,1024,512]{2,1,0:T(8,128)} %get-tuple-element.16.rb_ref, bf16[2048,512]{1,0:T(8,128)(2,1)} %get-tuple-element.17.ct_hi, ...), custom_call_target="tpu_custom_call" | custom-call | flops 12884901888 | bytes 29360128 | tf_op jit(solution)/shard_map/pallas_call | solution.py:918
Async XLA Ops:
  0.6 212.7 %copy-start = (f32[1024,512]{1,0:T(8,128)S(1)}, f32[1024,512]{1,0:T(8,128)}, u32[]{:S(2)}) copy-start(f32[1024,512]{1,0:T(8,128)} %a_ref.1) | copy-start | bytes 6291460
  213.3 1.6 copy-start.1
  214.9 0.8 copy-start.2
  215.7 0.8 copy-start.3
  216.6 0.7 copy-start.4

commit v4 on v1

--- a/solution.py
+++ b/solution.py
@@ -161,19 +161,27 @@
                 def _():
                     direct(view, c).start()
 
-    def far_b(src):
-        return send(src, raw_b.at[3], far_s.at[1], far_r.at[1], neighbour(-1))
-
-    def far_a(src):
-        return send(src, raw_a.at[3], far_s.at[0], far_r.at[0], neighbour(1))
-
-    @pl.when(odd)
-    def _():
-        far_b(b_hbm).start()
+    raws = (raw_a, raw_b)
+
+    def quarter(j):
+        return pl.ds(j * band, band)
+
+    def far(view, j, src=None):
+        raw = raws[view]
+        src = raw.at[1] if src is None else src
+        return send(
+            src.at[quarter(j)], raw.at[3, quarter(j)], far_s.at[view, j], far_r.at[view, j],
+            neighbour(1 - 2 * view),
+        )
+
+    def far_take(view):
+        for j in range(BANDS):
+            far(view, j).wait_recv()
 
     @pl.when(even)
     def _():
-        far_a(a_hbm).start()
+        for j in range(BANDS):
+            far(0, j, a_hbm).start()
 
     load_b.wait()
     load_a.wait()
@@ -440,9 +448,8 @@
         for view, st in ((1, st_b), (0, st_a)):
             landed(st.at[slot], stf_r.at[view, slot], stf_s.at[view, slot])
 
-    @pl.when(odd)
-    def _():
-        far_a(a_hbm).wait_recv()
+    def fourth():
+        far_take(0)
 
         def fourth_tile(c, carry):
             turn_a(3, c, BANDS)
@@ -456,18 +463,11 @@
     def early(j):
         if j < HOPS:
             sum_step(0, j)
-            when(odd, sum_step, 3, j)
-        elif j == 4:
-            end_0()
-            gather(2, -1)
-            when(odd, end_3_odd)
-        elif j == 5:
-            gather(2, 0)
-            when(even, hand_take, 3)
-            gather(3, -1)
         else:
-            gather(2, j - 5)
-            gather(3, j - 6)
+            when(odd, sum_step, 3, j - HOPS)
+            if j == HOPS:
+                end_0()
+            gather(2, j - HOPS - 1)
 
     for c in range(BANDS):
         for j in (2 * c, 2 * c + 1):
@@ -478,9 +478,10 @@
                         landed(relay.at[j], rel_r.at[j], rel_s.at[j])
                         from_relay(view, j).start()
 
-            for view in (1, 0):
-                direct(view, j).wait_recv()
-                forward(view, j).start()
+            direct(1, j).wait_recv()
+            forward(1, j).start()
+            direct(0, j).wait_recv()
+            when(odd, lambda: forward(0, j).start())
             early(j)
         take_b(1, c)
         add_tile(1, c, at_hi, at_lo, False)
@@ -496,17 +497,26 @@
             forward(1, j).wait_recv()
         take_b(2, c)
         add_tile(2, c, at_hi, at_lo, False)
+        if c == 1:
+            when(odd, fourth)
+
+    @pl.when(even)
+    def _():
+        for j in range(PARTS):
+            forward(0, j).start()
 
     @pl.when(odd)
     def _():
-        for j in range(PARTS):
-            forward(0, j).wait_recv()
+        for j in range(BANDS):
+            far(1, j, b_hbm).start()
+
+    def late_start(j):
+        when(even, lambda: far(1, j).start())
+        when(odd, lambda: far(0, j).start())
 
     for t in (1, 2):
         sum_start(t, 0)
     when(even, sum_start, 3, 0)
-    when(even, far_b(raw_b.at[1]).start)
-    when(odd, far_a(raw_a.at[1]).start)
 
     squares[...] = jnp.zeros_like(squares)
     columns[...] = jnp.zeros_like(columns)
@@ -581,33 +591,29 @@
         if r < 3:
             loss_copy(r + 1).start()
 
-    gather(2, 3)
-    gather(3, 2)
-    grow(0, 0, 0)
-    gather(3, 3)
-    for t in (1, 2):
-        sum_step(t, 0)
-    when(even, sum_step, 3, 0)
-    grow(1, 0, 0)
-    for t in (1, 2):
-        sum_step(t, 1)
-    when(even, sum_step, 3, 1)
-    far_b_here = far_b(raw_b.at[1])
-    far_a_here = far_a(raw_a.at[1])
-
-    @pl.when(even)
-    def _():
-        far_b_here.wait_recv()
-        grow(0, 3, 3)
-
-    when(odd, grow, 1, 3, 6)
-    for s in (2, 3):
+    def sum_round(s):
         for t in (1, 2):
             sum_step(t, s)
         when(even, sum_step, 3, s)
+        late_start(s)
+
+    when(odd, end_3_odd)
+    gather(2, 3)
+    grow(0, 0, 0)
+    sum_round(0)
+    when(even, hand_take, 3)
+    gather(3, -1)
+    grow(1, 0, 0)
+    sum_round(1)
+    gather(3, 0)
+    sum_round(2)
+    gather(3, 1)
+    sum_round(3)
+    gather(3, 2)
     end_1()
     end_2()
     gather(0, -1)
+    gather(3, 3)
     when(even, end_3_even)
     loss_part()
     for d in range(1, NZ):
@@ -627,11 +633,24 @@
     loss_start()
     gather(4, 1)
     gather(1, 2)
+
+    @pl.when(even)
+    def _():
+        far_take(1)
+        grow(0, 3, 3)
+
+    when(odd, grow, 1, 3, 6)
     gather(0, 3)
     grow(0, 1 + y_lo, lane_tile[0])
     loss_step(0)
     gather(4, 2)
     gather(1, 3)
+
+    @pl.when(odd)
+    def _():
+        for j in range(PARTS):
+            forward(0, j).wait_recv()
+
     grow(1, 1 + y_lo, lane_tile[1])
     loss_step(1)
     gather(4, 3)
@@ -644,12 +663,12 @@
 
     @pl.when(odd)
     def _():
-        far_b_here.wait_recv()
+        far_take(1)
         grow(0, 3, 3)
 
     @pl.when(even)
     def _():
-        far_a_here.wait_recv()
+        far_take(0)
         grow(1, 3, 6)
 
     loss_ref[0, 0] = jnp.sum(l_send[4]) * (1.0 / features)
@@ -690,8 +709,9 @@
         for c in range(PARTS):
             direct(view, c).wait_send()
             forward(view, c).wait_send()
-    far_a(a_hbm).wait_send()
-    far_b(b_hbm).wait_send()
+    for view in (0, 1):
+        for j in range(BANDS):
+            far(view, j).wait_send()
 
     @pl.when(seam)
     def _():
@@ -781,7 +801,7 @@
             dma((2, BANDS)),
             dma((2, PARTS)), dma((2, PARTS)),
             dma((2, PARTS)), dma((2, PARTS)),
-            dma((2,)), dma((2,)),
+            dma((2, BANDS)), dma((2, BANDS)),
             dma((PARTS // 2,)), dma((PARTS // 2,)),
             dma((NZ,)), dma((NZ,)),
             dma(()), dma(()),

time: 214 us -> 220 us (1.028)
  Pallas kernels: 203 us -> 211 us
    pallas_call x1, Pallas kernels: 203 us -> 211 us  [local(): pl.pallas_call(kernel, out_shape=(jax.ShapeDtypeStruct((rows, width), F32...]
where the time goes in v4:
time: 220 us; the launch traced here: 218 us
  Pallas kernels  211 us (96%)
  local copies, waits for them, and re-layouts  4.55 us (2%)
  between operations  2.47 us (1%)
    pallas_call x1, Pallas kernels, local(): pl.pallas_call(kernel, out_shape=(jax.ShapeDtypeStruct((rows, width), F32...  211 us
    unnamed x4, local copies, waits for them, and re-layouts  4.55 us

profile of v4, /device:TPU:16, one launch (start us, length us, event | category | flops | bytes accessed | tf_op | source)
XLA Modules:
  0.0 217.6 jit_solution(16424370670329812319)
XLA Ops:
  0.6 210.6 %shard_map.49 = (f32[1024,512]{1,0:T(8,128)}, f32[1024,512]{1,0:T(8,128)}, f32[1,1]{1,0:T(1,128)}) custom-call(f32[1024,512]{1,0:T(8,128)} %a_hbm.1, f32[1024,512]{1,0:T(8,128)} %b_hbm.1), custom_call_target="tpu_custom_call" | custom-call | flops 19327352832 | bytes 8388608 | tf_op jit(solution)/shard_map/pallas_call | solution.py:763
  211.2 0.0 copy-start
  211.2 3.2 %copy.8 = f32[1024,512]{1,0:T(8,128)} copy(f32[1024,512]{1,0:T(8,128)} %get-tuple-element.12) | data formatting | bytes 4194304
  214.4 0.0 copy-done
  214.4 1.3 copy.9
Async XLA Ops:
  211.2 3.2 %copy-start = (f32[1024,512]{1,0:T(8,128)S(1)}, f32[1024,512]{1,0:T(8,128)}, u32[]{:S(2)}) copy-start(f32[1024,512]{1,0:T(8,128)} %get-tuple-element.13) | copy-start | bytes 6291460

commit v5 on v4

--- a/solution.py
+++ b/solution.py
@@ -460,14 +460,23 @@
         lax.fori_loop(0, BANDS, fourth_tile, 0)
         sum_start(3, 0)
 
+    when(odd, fourth)
+
     def early(j):
         if j < HOPS:
             sum_step(0, j)
+            when(odd, sum_step, 3, j)
+        elif j == 4:
+            end_0()
+            gather(2, -1)
+            when(odd, end_3_odd)
+        elif j == 5:
+            gather(2, 0)
+            when(even, hand_take, 3)
+            gather(3, -1)
         else:
-            when(odd, sum_step, 3, j - HOPS)
-            if j == HOPS:
-                end_0()
-            gather(2, j - HOPS - 1)
+            gather(2, j - 5)
+            gather(3, j - 6)
 
     for c in range(BANDS):
         for j in (2 * c, 2 * c + 1):
@@ -482,6 +491,8 @@
             forward(1, j).start()
             direct(0, j).wait_recv()
             when(odd, lambda: forward(0, j).start())
+            if j >= BANDS:
+                when(odd, lambda: far(1, j - BANDS, b_hbm).start())
             early(j)
         take_b(1, c)
         add_tile(1, c, at_hi, at_lo, False)
@@ -497,18 +508,11 @@
             forward(1, j).wait_recv()
         take_b(2, c)
         add_tile(2, c, at_hi, at_lo, False)
-        if c == 1:
-            when(odd, fourth)
 
     @pl.when(even)
     def _():
         for j in range(PARTS):
             forward(0, j).start()
-
-    @pl.when(odd)
-    def _():
-        for j in range(BANDS):
-            far(1, j, b_hbm).start()
 
     def late_start(j):
         when(even, lambda: far(1, j).start())
@@ -597,23 +601,25 @@
         when(even, sum_step, 3, s)
         late_start(s)
 
-    when(odd, end_3_odd)
     gather(2, 3)
+    gather(3, 2)
     grow(0, 0, 0)
+    gather(3, 3)
     sum_round(0)
-    when(even, hand_take, 3)
-    gather(3, -1)
     grow(1, 0, 0)
     sum_round(1)
-    gather(3, 0)
+
+    @pl.when(even)
+    def _():
+        far_take(1)
+        grow(0, 3, 3)
+
+    when(odd, grow, 1, 3, 6)
     sum_round(2)
-    gather(3, 1)
     sum_round(3)
-    gather(3, 2)
     end_1()
     end_2()
     gather(0, -1)
-    gather(3, 3)
     when(even, end_3_even)
     loss_part()
     for d in range(1, NZ):
@@ -633,13 +639,6 @@
     loss_start()
     gather(4, 1)
     gather(1, 2)
-
-    @pl.when(even)
-    def _():
-        far_take(1)
-        grow(0, 3, 3)
-
-    when(odd, grow, 1, 3, 6)
     gather(0, 3)
     grow(0, 1 + y_lo, lane_tile[0])
     loss_step(0)

time: 220 us -> 224 us (1.018)
  Pallas kernels: 211 us -> 214 us
    pallas_call x1, Pallas kernels: 211 us -> 214 us  [local(): pl.pallas_call(kernel, out_shape=(jax.ShapeDtypeStruct((rows, width), F32...]
where the time goes in v5:
time: 224 us; the launch traced here: 221 us
  Pallas kernels  214 us (96%)
  local copies, waits for them, and re-layouts  4.55 us (2%)
  between operations  2.47 us (1%)
    pallas_call x1, Pallas kernels, local(): pl.pallas_call(kernel, out_shape=(jax.ShapeDtypeStruct((rows, width), F32...  214 us
    unnamed x4, local copies, waits for them, and re-layouts  4.55 us

profile of v5, /device:TPU:16, one launch (start us, length us, event | category | flops | bytes accessed | tf_op | source)
XLA Modules:
  0.0 221.0 jit_solution(18196461789306425441)
XLA Ops:
  0.6 214.0 %shard_map.49 = (f32[1024,512]{1,0:T(8,128)}, f32[1024,512]{1,0:T(8,128)}, f32[1,1]{1,0:T(1,128)}) custom-call(f32[1024,512]{1,0:T(8,128)} %a_hbm.1, f32[1024,512]{1,0:T(8,128)} %b_hbm.1), custom_call_target="tpu_custom_call" | custom-call | flops 19327352832 | bytes 8388608 | tf_op jit(solution)/shard_map/pallas_call | solution.py:762
  214.6 0.0 copy-start
  214.6 3.2 %copy.8 = f32[1024,512]{1,0:T(8,128)} copy(f32[1024,512]{1,0:T(8,128)} %get-tuple-element.12) | data formatting | bytes 4194304
  217.9 0.0 copy-done
  217.9 1.3 copy.9
Async XLA Ops:
  214.6 3.2 %copy-start = (f32[1024,512]{1,0:T(8,128)S(1)}, f32[1024,512]{1,0:T(8,128)}, u32[]{:S(2)}) copy-start(f32[1024,512]{1,0:T(8,128)} %get-tuple-element.13) | copy-start | bytes 6291460

commit v6 on v1

--- a/solution.py
+++ b/solution.py
@@ -41,8 +41,8 @@
 def kernel(
     a_hbm, b_hbm, ga_hbm, gb_hbm, loss_ref,
     raw_a, raw_b, at_hi, at_lo, b_hi, b_lo, tiles, rs_p, rs_m, y_recv, fin, cfull, c_hi, c_lo,
-    g_a, g_b, relay, st_z, st_y, st_a, st_b, squares, columns, means, l_z, l_send, l_recv,
-    in_sem, out_sem, direct_s, direct_r, fwd_s, fwd_r, far_s, far_r, rel_s, rel_r,
+    g_a, g_b, relay, relay_far, st_z, st_y, st_a, st_b, squares, columns, means, l_z, l_send, l_recv,
+    in_sem, out_sem, direct_s, direct_r, fwd_s, fwd_r, far_s, far_r, rel_s, rel_r, rel_far_s, rel_far_r,
     stz_s, stz_r, sty_s, sty_r, stf_s, stf_r, rs_s, rs_r, y_s, y_r, hand_s, hand_r,
     ag_s, ag_r, ay_s, ay_r, lz_s, lz_r, loss_s, loss_r,
 ):
@@ -73,8 +73,8 @@
     def at_z(z_other):
         return {"batch": z_other * 2 + y_lo, "feat": feat}
 
-    def at_xy(x_other, y_other):
-        f = lax.div(y_other, 2) * (2 * NX) + x_other * 2 + core
+    def at_xy(x_other, y_other, core_other):
+        f = lax.div(y_other, 2) * (2 * NX) + x_other * 2 + core_other
         return {"batch": z * 2 + lax.rem(y_other, 2), "feat": f}
 
     def neighbour(steps):
@@ -115,12 +115,13 @@
     @pl.when(seam)
     def _():
         for friend in (
-            at_xy(mirror_x, mod(y - 1, NY)), at_xy(mirror_x, mod(y + 1, NY)),
-            at_xy(x, mod(y - 1, NY)), at_xy(x, mod(y + 1, NY)),
+            at_xy(mirror_x, mod(y - 1, NY), core), at_xy(mirror_x, mod(y + 1, NY), core),
+            at_xy(x, mod(y - 1, NY), core), at_xy(x, mod(y + 1, NY), core),
+            at_xy(x, mod(y - 1, NY), 1 - core), at_xy(x, mod(y + 1, NY), 1 - core),
         ):
             pl.semaphore_signal(barrier, inc=1, device_id=friend, device_id_type=MESH)
 
-    pl.semaphore_wait(barrier, jnp.where(seam, len(friends) + 4, len(friends)))
+    pl.semaphore_wait(barrier, jnp.where(seam, len(friends) + 6, len(friends)))
 
 
     def piece(c):
@@ -137,7 +138,7 @@
         src = (a_hbm, b_hbm)[view]
         return send(
             src.at[piece(c)], relay.at[c - PARTS // 2], direct_s.at[view, c],
-            rel_r.at[c - PARTS // 2], at_xy(mirror_x, mod(y - 1, NY)),
+            rel_r.at[c - PARTS // 2], at_xy(mirror_x, mod(y - 1, NY), core),
         )
 
     def from_relay(view, r):
@@ -145,7 +146,7 @@
         c = r + PARTS // 2
         return send(
             relay.at[r], raw.at[1, piece(c)], rel_s.at[r], direct_r.at[view, c],
-            at_xy(x, mod(y - 1, NY)),
+            at_xy(x, mod(y - 1, NY), core),
         )
 
     for c in (0, 4, 1, 5, 2, 6, 3, 7):
@@ -161,19 +162,59 @@
                 def _():
                     direct(view, c).start()
 
-    def far_b(src):
-        return send(src, raw_b.at[3], far_s.at[1], far_r.at[1], neighbour(-1))
-
-    def far_a(src):
-        return send(src, raw_a.at[3], far_s.at[0], far_r.at[0], neighbour(1))
+    raws = (raw_a, raw_b)
+    late = ((0, odd, last_x, first_x), (1, even, first_x, last_x))
+
+    def far(view, src, here):
+        raw = raws[view]
+        return send(
+            src.at[here], raw.at[3, here], far_s.at[view], far_r.at[view], neighbour(1 - 2 * view)
+        )
+
+    def left_here(src, s_sem):
+        send(src, src, s_sem, sty_r, other_core).wait_send()
+
+    def far_take(view):
+        landed(raws[view].at[3], far_r.at[view], far_s.at[view])
+
+    def late_start(view, side, leaves, j):
+        raw = raws[view]
+        if j < PARTS // 2:
+            @pl.when(side)
+            def _():
+                far(view, raw.at[1], piece(j)).start()
+        else:
+            @pl.when(jnp.logical_and(side, leaves))
+            def _():
+                send(
+                    raw.at[1, piece(j)], relay_far.at[j - PARTS // 2], far_s.at[view],
+                    rel_far_r.at[j - PARTS // 2], at_xy(mirror_x, mod(y - 1, NY), core),
+                ).start()
+
+            @pl.when(jnp.logical_and(side, jnp.logical_not(leaves)))
+            def _():
+                far(view, raw.at[1], piece(j)).start()
+
+    def late_out(view, r):
+        return send(
+            relay_far.at[r], raws[view].at[3, piece(r + PARTS // 2)], rel_far_s.at[r], far_r.at[view],
+            at_xy(x, mod(y - 1, NY), 1 - core),
+        )
+
+    def late_pass(r):
+        for view, side, leaves, enters in late:
+            @pl.when(jnp.logical_and(side, enters))
+            def _():
+                landed(relay_far.at[r], rel_far_r.at[r], rel_far_s.at[r])
+                late_out(view, r).start()
 
     @pl.when(odd)
     def _():
-        far_b(b_hbm).start()
+        far(1, b_hbm, pl.ds(0, rows)).start()
 
     @pl.when(even)
     def _():
-        far_a(a_hbm).start()
+        far(0, a_hbm, pl.ds(0, rows)).start()
 
     load_b.wait()
     load_a.wait()
@@ -442,7 +483,7 @@
 
     @pl.when(odd)
     def _():
-        far_a(a_hbm).wait_recv()
+        far_take(0)
 
         def fourth_tile(c, carry):
             turn_a(3, c, BANDS)
@@ -481,6 +522,8 @@
             for view in (1, 0):
                 direct(view, j).wait_recv()
                 forward(view, j).start()
+                _, side, leaves, _ = late[view]
+                late_start(view, side, leaves, j)
             early(j)
         take_b(1, c)
         add_tile(1, c, at_hi, at_lo, False)
@@ -505,8 +548,6 @@
     for t in (1, 2):
         sum_start(t, 0)
     when(even, sum_start, 3, 0)
-    when(even, far_b(raw_b.at[1]).start)
-    when(odd, far_a(raw_a.at[1]).start)
 
     squares[...] = jnp.zeros_like(squares)
     columns[...] = jnp.zeros_like(columns)
@@ -588,16 +629,18 @@
     for t in (1, 2):
         sum_step(t, 0)
     when(even, sum_step, 3, 0)
+    late_pass(0)
+    late_pass(1)
     grow(1, 0, 0)
     for t in (1, 2):
         sum_step(t, 1)
     when(even, sum_step, 3, 1)
-    far_b_here = far_b(raw_b.at[1])
-    far_a_here = far_a(raw_a.at[1])
+    late_pass(2)
+    late_pass(3)
 
     @pl.when(even)
     def _():
-        far_b_here.wait_recv()
+        far_take(1)
         grow(0, 3, 3)
 
     when(odd, grow, 1, 3, 6)
@@ -644,12 +687,12 @@
 
     @pl.when(odd)
     def _():
-        far_b_here.wait_recv()
+        far_take(1)
         grow(0, 3, 3)
 
     @pl.when(even)
     def _():
-        far_a_here.wait_recv()
+        far_take(0)
         grow(1, 3, 6)
 
     loss_ref[0, 0] = jnp.sum(l_send[4]) * (1.0 / features)
@@ -690,8 +733,13 @@
         for c in range(PARTS):
             direct(view, c).wait_send()
             forward(view, c).wait_send()
-    far_a(a_hbm).wait_send()
-    far_b(b_hbm).wait_send()
+    for view, side, leaves, enters in late:
+        left_here(raws[view].at[3], far_s.at[view])
+
+        @pl.when(jnp.logical_and(side, enters))
+        def _():
+            for r in range(PARTS // 2):
+                late_out(view, r).wait_send()
 
     @pl.when(seam)
     def _():
@@ -767,6 +815,7 @@
             pltpu.VMEM((rows, width), F32),
             pltpu.VMEM((rows, width), F32),
             pltpu.VMEM((PARTS // 2, part, width), F32),
+            pltpu.VMEM((PARTS // 2, part, width), F32),
             pltpu.VMEM((NZ, 8, width), F32),
             pltpu.VMEM((2, 8, width), F32),
             pltpu.VMEM((4, 8, width), F32),
@@ -782,6 +831,7 @@
             dma((2, PARTS)), dma((2, PARTS)),
             dma((2, PARTS)), dma((2, PARTS)),
             dma((2,)), dma((2,)),
+            dma((PARTS // 2,)), dma((PARTS // 2,)),
             dma((PARTS // 2,)), dma((PARTS // 2,)),
             dma((NZ,)), dma((NZ,)),
             dma(()), dma(()),

time: 214 us -> 237 us (1.11)
  Pallas kernels: 203 us -> 226 us
    pallas_call x1, Pallas kernels: 203 us -> 226 us  [local(): pl.pallas_call(kernel, out_shape=(jax.ShapeDtypeStruct((rows, width), F32...]
where the time goes in v6:
time: 237 us; the launch traced here: 233 us
  Pallas kernels  226 us (95%)
  local copies, waits for them, and re-layouts  4.55 us (2%)
  between operations  2.47 us (1%)
    pallas_call x1, Pallas kernels, local(): pl.pallas_call(kernel, out_shape=(jax.ShapeDtypeStruct((rows, width), F32...  226 us

profile of v6, /device:TPU:16, one launch (start us, length us, event | category | flops | bytes accessed | tf_op | source)
XLA Modules:
  0.0 233.3 jit_solution(17809106281585001407)
XLA Ops:
  0.6 226.3 %shard_map.49 = (f32[1024,512]{1,0:T(8,128)}, f32[1024,512]{1,0:T(8,128)}, f32[1,1]{1,0:T(1,128)}) custom-call(f32[1024,512]{1,0:T(8,128)} %a_hbm.1, f32[1024,512]{1,0:T(8,128)} %b_hbm.1), custom_call_target="tpu_custom_call" | custom-call | flops 19327352832 | bytes 8388608 | tf_op jit(solution)/shard_map/pallas_call | solution.py:791
  227.0 0.0 copy-start
  227.0 3.2 %copy.8 = f32[1024,512]{1,0:T(8,128)} copy(f32[1024,512]{1,0:T(8,128)} %get-tuple-element.12) | data formatting | bytes 4194304
  230.2 0.0 copy-done
  230.2 1.3 copy.9
Async XLA Ops:
  227.0 3.2 %copy-start = (f32[1024,512]{1,0:T(8,128)S(1)}, f32[1024,512]{1,0:T(8,128)}, u32[]{:S(2)}) copy-start(f32[1024,512]{1,0:T(8,128)} %get-tuple-element.13) | copy-start | bytes 6291460

commit v7 on v1

--- a/solution.py
+++ b/solution.py
@@ -19,6 +19,7 @@
 NY = 4
 NF = 16
 PARTS = 8
+AHEAD = 3
 BANDS = 4
 HOPS = 4
 
@@ -148,7 +149,7 @@
             at_xy(x, mod(y - 1, NY)),
         )
 
-    for c in (0, 4, 1, 5, 2, 6, 3, 7):
+    def piece_start(c):
         for view, edge in ((1, first_x), (0, last_x)):
             if c < PARTS // 2:
                 direct(view, c).start()
@@ -160,6 +161,9 @@
                 @pl.when(jnp.logical_not(edge))
                 def _():
                     direct(view, c).start()
+
+    for c in range(AHEAD):
+        piece_start(c)
 
     def far_b(src):
         return send(src, raw_b.at[3], far_s.at[1], far_r.at[1], neighbour(-1))
@@ -471,16 +475,19 @@
 
     for c in range(BANDS):
         for j in (2 * c, 2 * c + 1):
-            if j < PARTS // 2:
+            r = j - AHEAD
+            if 0 <= r < PARTS // 2:
                 for view, edge in ((1, last_x), (0, first_x)):
                     @pl.when(edge)
                     def _():
-                        landed(relay.at[j], rel_r.at[j], rel_s.at[j])
-                        from_relay(view, j).start()
+                        landed(relay.at[r], rel_r.at[r], rel_s.at[r])
+                        from_relay(view, r).start()
 
             for view in (1, 0):
                 direct(view, j).wait_recv()
                 forward(view, j).start()
+            if j + AHEAD < PARTS:
+                piece_start(j + AHEAD)
             early(j)
         take_b(1, c)
         add_tile(1, c, at_hi, at_lo, False)

time: 214 us -> 201 us (0.939); the launches traced: 210 us -> 200 us
  Pallas kernels: 203 us -> 193 us
    pallas_call x1, Pallas kernels: 203 us -> 193 us  [local(): pl.pallas_call(kernel, out_shape=(jax.ShapeDtypeStruct((rows, width), F32...]
where the time goes in v7:
time: 201 us; the launch traced here: 200 us
  Pallas kernels  193 us (96%)
  local copies, waits for them, and re-layouts  4.55 us (2%)
  between operations  2.47 us (1%)
    pallas_call x1, Pallas kernels, local(): pl.pallas_call(kernel, out_shape=(jax.ShapeDtypeStruct((rows, width), F32...  193 us
    unnamed x4, local copies, waits for them, and re-layouts  4.55 us

profile of v7, /device:TPU:16, one launch (start us, length us, event | category | flops | bytes accessed | tf_op | source)
XLA Modules:
  0.0 200.2 jit_solution(13932739587774048589)
XLA Ops:
  0.6 193.1 %shard_map.49 = (f32[1024,512]{1,0:T(8,128)}, f32[1024,512]{1,0:T(8,128)}, f32[1,1]{1,0:T(1,128)}) custom-call(f32[1024,512]{1,0:T(8,128)} %a_hbm.1, f32[1024,512]{1,0:T(8,128)} %b_hbm.1), custom_call_target="tpu_custom_call" | custom-call | flops 19327352832 | bytes 8388608 | tf_op jit(solution)/shard_map/pallas_call | solution.py:750
  193.8 0.0 copy-start
  193.8 3.2 %copy.8 = f32[1024,512]{1,0:T(8,128)} copy(f32[1024,512]{1,0:T(8,128)} %get-tuple-element.12) | data formatting | bytes 4194304
  197.0 0.0 copy-done
  197.0 1.3 copy.9
Async XLA Ops:
  193.8 3.2 %copy-start = (f32[1024,512]{1,0:T(8,128)S(1)}, f32[1024,512]{1,0:T(8,128)}, u32[]{:S(2)}) copy-start(f32[1024,512]{1,0:T(8,128)} %get-tuple-element.13) | copy-start | bytes 6291460

commit v8 on v7

--- a/solution.py
+++ b/solution.py
@@ -19,7 +19,7 @@
 NY = 4
 NF = 16
 PARTS = 8
-AHEAD = 3
+AHEAD = 2
 BANDS = 4
 HOPS = 4
 
@@ -475,7 +475,7 @@
 
     for c in range(BANDS):
         for j in (2 * c, 2 * c + 1):
-            r = j - AHEAD
+            r = j - (PARTS // 2 - 1)
             if 0 <= r < PARTS // 2:
                 for view, edge in ((1, last_x), (0, first_x)):
                     @pl.when(edge)

time: 201 us -> 206 us (1.025)
  Pallas kernels: 193 us -> 197 us
    pallas_call x1, Pallas kernels: 193 us -> 197 us  [local(): pl.pallas_call(kernel, out_shape=(jax.ShapeDtypeStruct((rows, width), F32...]
where the time goes in v8:
time: 206 us; the launch traced here: 204 us
  Pallas kernels  197 us (96%)
  local copies, waits for them, and re-layouts  4.55 us (2%)
  between operations  2.47 us (1%)
    pallas_call x1, Pallas kernels, local(): pl.pallas_call(kernel, out_shape=(jax.ShapeDtypeStruct((rows, width), F32...  197 us
    unnamed x4, local copies, waits for them, and re-layouts  4.55 us

profile of v8, /device:TPU:16, one launch (start us, length us, event | category | flops | bytes accessed | tf_op | source)
XLA Modules:
  0.0 203.5 jit_solution(5790954960151720466)
XLA Ops:
  0.6 196.5 %shard_map.49 = (f32[1024,512]{1,0:T(8,128)}, f32[1024,512]{1,0:T(8,128)}, f32[1,1]{1,0:T(1,128)}) custom-call(f32[1024,512]{1,0:T(8,128)} %a_hbm.1, f32[1024,512]{1,0:T(8,128)} %b_hbm.1), custom_call_target="tpu_custom_call" | custom-call | flops 19327352832 | bytes 8388608 | tf_op jit(solution)/shard_map/pallas_call | solution.py:750
  197.1 0.0 copy-start
  197.1 3.2 %copy.8 = f32[1024,512]{1,0:T(8,128)} copy(f32[1024,512]{1,0:T(8,128)} %get-tuple-element.12) | data formatting | bytes 4194304
  200.4 0.0 copy-done
  200.4 1.3 copy.9
Async XLA Ops:
  197.1 3.2 %copy-start = (f32[1024,512]{1,0:T(8,128)S(1)}, f32[1024,512]{1,0:T(8,128)}, u32[]{:S(2)}) copy-start(f32[1024,512]{1,0:T(8,128)} %get-tuple-element.13) | copy-start | bytes 6291460
